TPU v7x, 1024 devices: a whole 4x8x16 slice. The times are simulated.
1024 devices in a mesh: group: 256 (over z, y, core), member: 4 (over x).
Axes of the slice: x: 4, y: 8, z: 16, core: 2. Of those that a mesh axis runs over, the one named last changes fastest.
Arguments:
- targets: bfloat16 [262144, 768], P(('group', 'member')), may hold values from -6 to 6
- neighbors: int32 [262144, 25], P(('group', 'member')), may hold values from 0 to 511, as said below
- hot_table: bfloat16 [2048, 768], P('member'), may hold values from -6 to 6
- hot_req: int32 [256, 4, 4, 64], P('group', 'member'), may hold values from 0 to 511
- hot_count: int32 [256, 4, 4], P('group', 'member'), may hold values from 1 to 64, as said below
- cold_table: bfloat16 [131072, 768], P('group'), may hold values from -6 to 6
- cold_owner: int32 [256, 4, 256], P('group', 'member'), may hold values from 0 to 255, as said below
- cold_row: int32 [256, 4, 256], P('group', 'member'), may hold values from 0 to 511
- w_self: bfloat16 [768, 1024], replicated, may hold values from -0.21875 to 0.21875
- w_neigh: bfloat16 [768, 1024], replicated, may hold values from -1 to 1
- bias: float32 [1024], replicated, may hold values from -3 to 3
Outputs:
- embedded: bfloat16 [262144, 1024], P(('group', 'member'))
Inputs may be any that keep to these rules, and one draw needn't show every extreme that they name: `cold_owner`: each device asks exactly 2 rows of one owner group, the same group for all devices with the same member index, none of one other group and one of every remaining group. `hot_count`: in every group one member receives 64 live slots from each member of the group. `neighbors`: an entry below 256 names slot n % 64 of peer n // 64 and only live slots; others name cold request n - 256.
All inputs are finite; a program needn't handle non-finite values.
Results may differ from a plain program's by a relative error of at most 0.0039.
Values may be sent and summed in bfloat16 or wider, within the bound.
A program may use at most 128 MiB of HBM per device.

v0:
```python
import jax
import jax.numpy as jnp
from jax import lax
from jax.sharding import PartitionSpec as P

FANOUT = 25
CCAP = 2


def from_partner(array, axis, distance):
    return lax.ppermute(array, axis, [(i, i ^ 1 << distance) for i in range(lax.axis_size(axis))])


def relay(buffer, mover):
    groups = buffer.shape[0]
    depth = groups.bit_length() - 1
    levels = list(range(depth))
    tail = buffer.shape[1:]
    for bit_index in levels:
        shaped = buffer.reshape((groups >> bit_index + 1, 2, 1 << bit_index) + tail)
        arrived = mover(shaped[:, 1], bit_index)
        buffer = jnp.stack([shaped[:, 0], arrived], axis=1).reshape(buffer.shape)
    return buffer


def move_ids(buffer, bit_index):
    return from_partner(buffer, "group", bit_index)


def move_rows(buffer, bit_index):
    return from_partner(buffer, "group", bit_index)


def per_device(
    targets,
    neighbors,
    hot_table,
    hot_req,
    hot_count,
    cold_table,
    cold_owner,
    cold_row,
    w_self,
    w_neigh,
    bias,
):
    members = hot_req.shape[2]
    hot_slots = hot_req.shape[3]
    width = hot_table.shape[1]
    groups = lax.axis_size("group")
    myself = lax.axis_index("group")
    asked_hot = hot_req.reshape(members, hot_slots)
    rows_out = jnp.take(
        hot_table,
        lax.all_to_all(asked_hot, "member", split_axis=0, concat_axis=0, tiled=True),
        axis=0,
    )
    hot_rows = lax.all_to_all(rows_out, "member", split_axis=0, concat_axis=0, tiled=True)
    hot_rows = hot_rows.reshape(members * hot_slots, width)
    live = hot_count.reshape(members, 1)
    keep = (jnp.arange(hot_slots, dtype=jnp.int32)[None, :] < live).reshape(-1)
    hot_rows = jnp.where(keep[:, None], hot_rows, jnp.zeros_like(hot_rows))
    owners = cold_owner.reshape(-1)
    wanted = cold_row.reshape(-1)
    requests = owners.shape[0]
    position = jnp.arange(requests, dtype=jnp.int32)
    same_owner = owners[:, None] == owners[None, :]
    earlier = position[:, None] > position[None, :]
    rank = jnp.sum((same_owner & earlier).astype(jnp.int32), axis=1)
    relative = jnp.bitwise_xor(owners, myself)
    flat_slot = relative * CCAP + rank
    id_buffer = jnp.zeros((groups * CCAP,), jnp.int32).at[flat_slot].set(wanted)
    asked_cold = relay(id_buffer.reshape(groups, CCAP), move_ids)
    served = jnp.take(cold_table, asked_cold.reshape(-1), axis=0).reshape(groups, CCAP, width)
    returned = relay(served, move_rows)
    cold_rows = jnp.take(returned.reshape(groups * CCAP, width), flat_slot, axis=0)
    self_part = jnp.dot(targets, w_self, preferred_element_type=jnp.float32)
    fetched = jnp.concatenate([hot_rows, cold_rows], axis=0)
    columns = jnp.arange(fetched.shape[0], dtype=jnp.int32)
    tallies = jnp.sum((neighbors[:, :, None] == columns[None, None, :]).astype(jnp.float32), axis=1)
    summed = jnp.dot(tallies.astype(jnp.bfloat16), fetched, preferred_element_type=jnp.float32)
    aggregate = (summed / FANOUT).astype(jnp.bfloat16)
    pre = self_part + jnp.dot(aggregate, w_neigh, preferred_element_type=jnp.float32)
    pre = pre + bias
    active = jnp.maximum(pre, 0.0)
    scale = lax.rsqrt(jnp.mean(active * active, axis=-1, keepdims=True) + 1e-06)
    return (active * scale).astype(jnp.bfloat16)


def solution(mesh):
    return jax.shard_map(
        per_device,
        mesh=mesh,
        in_specs=(
            P(("group", "member"), None),
            P(("group", "member"), None),
            P("member", None),
            P("group", "member", None, None),
            P("group", "member", None),
            P("group", None),
            P("group", "member", None),
            P("group", "member", None),
            P(),
            P(),
            P(),
        ),
        out_specs=P(("group", "member"), None),
        check_vma=False,
    )
```

profile of v0, /device:TPU:1, one launch (start us, length us, event | category | flops | bytes accessed | tf_op | source)
XLA Modules:
  0.0 264.7 jit_solution(13491508432843066495)
XLA Ops:
  0.0 1.0 convert_reduce_fusion.1
  1.7 1.6 scatter_custom_fusion
  3.6 16.1 %collective-permute-start = (s32[128,1,2]{2,0,1:T(8,128)S(1)}, s32[128,1,2]{2,0,1:T(8,128)S(1)}, u32[]{:S(2)}, u32[]{:S(2)}) collective-permute-start(s32[128,1,2]{2,0,1:T(8,128)S(1)} %bitcast.129), channel_id=1, source_target_pairs={{0,4},{4,0},{8,12},{12,8},{16,20},{20,16},{24,28},{28,24},{32,36},... | collective-permute-start | bytes 3080 | tf_op jit(solution)/shard_map/ppermute | solution.py:11
  20.7 1.9 collective-permute-start.1
  22.6 2.4 collective-permute-done.1
  25.4 1.9 collective-permute-start.2
  27.3 3.3 %collective-permute-done.2 = s32[32,4,2]{0,1,2:T(4,128)S(1)} collective-permute-done((s32[32,4,2]{0,1,2:T(4,128)S(1)}, s32[32,4,2]{0,1,2:T(4,128)S(1)}, u32[]{:S(2)}, u32[]{:S(2)}) %collective-permute-start.2) | collective-permute-done | bytes 1056 | tf_op jit(solution)/shard_map/ppermute | solution.py:11
  31.5 1.9 collective-permute-start.3
  33.4 6.5 %collective-permute-done.3 = s32[16,8,2]{1,2,0:T(2,128)S(1)} collective-permute-done((s32[16,8,2]{1,2,0:T(2,128)S(1)}, s32[16,8,2]{1,2,0:T(2,128)S(1)}, u32[]{:S(2)}, u32[]{:S(2)}) %collective-permute-start.3) | collective-permute-done | bytes 1056 | tf_op jit(solution)/shard_map/ppermute | solution.py:11
  40.0 1.9 collective-permute-start.4
  42.0 2.5 collective-permute-done.4
  44.6 1.9 collective-permute-start.5
  46.5 3.3 %collective-permute-done.5 = s32[4,32,2]{1,2,0:T(2,128)S(1)} collective-permute-done((s32[4,32,2]{1,2,0:T(2,128)S(1)}, s32[4,32,2]{1,2,0:T(2,128)S(1)}, u32[]{:S(2)}, u32[]{:S(2)}) %collective-permute-start.5) | collective-permute-done | bytes 1056 | tf_op jit(solution)/shard_map/ppermute | solution.py:11
  49.9 1.9 collective-permute-start.6
  51.8 6.3 %collective-permute-done.6 = s32[2,64,2]{1,2,0:T(2,128)S(1)} collective-permute-done((s32[2,64,2]{1,2,0:T(2,128)S(1)}, s32[2,64,2]{1,2,0:T(2,128)S(1)}, u32[]{:S(2)}, u32[]{:S(2)}) %collective-permute-start.6) | collective-permute-done | bytes 1056 | tf_op jit(solution)/shard_map/ppermute | solution.py:11
  58.3 6.6 %collective-permute-start.7 = (s32[1,128,2]{1,2,0:T(2,128)S(1)}, s32[1,128,2]{1,2,0:T(2,128)S(1)}, u32[]{:S(2)}, u32[]{:S(2)}) collective-permute-start(s32[1,128,2]{1,2,0:T(2,128)S(1)} %get-tuple-element.34), channel_id=1, source_target_pairs={{0,512},{4,516},{8,520},{12,524},{16,528},{20,532},{24,536},{28,54... | collective-permute-start | bytes 3080 | tf_op jit(solution)/shard_map/ppermute | solution.py:11
  64.9 6.4 %collective-permute-done.7 = s32[1,128,2]{1,2,0:T(2,128)S(1)} collective-permute-done((s32[1,128,2]{1,2,0:T(2,128)S(1)}, s32[1,128,2]{1,2,0:T(2,128)S(1)}, u32[]{:S(2)}, u32[]{:S(2)}) %collective-permute-start.7) | collective-permute-done | bytes 1056 | tf_op jit(solution)/shard_map/ppermute | solution.py:11
  71.6 2.0 gather_fusion.1
  74.1 0.9 copy.240
  75.1 1.0 broadcast_select_fusion
  76.6 10.3 %collective-permute-start.8 = (bf16[128,1,2,768]{3,2,0,1:T(2,128)(2,1)S(1)}, bf16[128,1,2,768]{3,2,0,1:T(2,128)(2,1)S(1)}, u32[]{:S(2)}, u32[]{:S(2)}) collective-permute-start(bf16[128,1,2,768]{3,2,0,1:T(2,128)(2,1)S(1)} %get-tuple-element.18), channel_id=1, source_target_pairs={{0,4},{4,0},{8,12},{12,8},{16,20},{20,16},{24,28},{28,24},{32,36},... | collective-permute-start | bytes 1179656 | tf_op jit(solution)/shard_map/ppermute | solution.py:11
  86.9 1.3 collective-permute-done.8
  88.2 1.1 fusion.12
  89.4 1.9 collective-permute-start.9
  91.3 10.3 %collective-permute-done.9 = bf16[64,2,2,768]{3,2,0,1:T(2,128)(2,1)S(1)} collective-permute-done((bf16[64,2,2,768]{3,2,0,1:T(2,128)(2,1)S(1)}, bf16[64,2,2,768]{3,2,0,1:T(2,128)(2,1)S(1)}, u32[]{:S(2)}, u32[]{:S(2)}) %collective-permute-start.9) | collective-permute-done | bytes 393248 | tf_op jit(solution)/shard_map/ppermute | solution.py:11
  101.6 1.1 pad_maximum_fusion
  103.5 1.9 collective-permute-start.10
  105.5 20.3 %collective-permute-done.10 = bf16[32,4,2,768]{3,2,1,0:T(2,128)(2,1)S(1)} collective-permute-done((bf16[32,4,2,768]{3,2,1,0:T(2,128)(2,1)S(1)}, bf16[32,4,2,768]{3,2,1,0:T(2,128)(2,1)S(1)}, u32[]{:S(2)}, u32[]{:S(2)}) %collective-permute-start.10) | collective-permute-done | bytes 393248 | tf_op jit(solution)/shard_map/ppermute | solution.py:11
  127.5 1.9 collective-permute-start.11
  129.5 3.6 %all-to-all-start = ((s32[4,1,64]{2,1,0:T(1,128)}), s32[4,1,64]{2,1,0:T(1,128)S(1)}, u32[]{:S(2)}, u32[]{:S(2)}) async-start(s32[4,1,64]{2,1,0:T(1,128)} %bitcast.1), calls=%async_computation | async-start | bytes 4096 | tf_op jit(solution)/shard_map/all_to_all | solution.py:55
  133.0 16.0 %collective-permute-done.11 = bf16[16,8,2,768]{3,2,1,0:T(2,128)(2,1)S(1)} collective-permute-done((bf16[16,8,2,768]{3,2,1,0:T(2,128)(2,1)S(1)}, bf16[16,8,2,768]{3,2,1,0:T(2,128)(2,1)S(1)}, u32[]{:S(2)}, u32[]{:S(2)}) %collective-permute-start.11) | collective-permute-done | bytes 393248 | tf_op jit(solution)/shard_map/ppermute | solution.py:11
  149.0 1.1 pad_maximum_fusion.2
  150.4 3.4 %collective-permute-start.12 = (bf16[8,16,2,768]{3,1,2,0:T(8,128)(2,1)S(1)}, bf16[8,16,2,768]{3,1,2,0:T(8,128)(2,1)S(1)}, u32[]{:S(2)}, u32[]{:S(2)}) collective-permute-start(bf16[8,16,2,768]{3,1,2,0:T(8,128)(2,1)S(1)} %get-tuple-element.12), channel_id=1, source_target_pairs={{0,64},{4,68},{8,72},{12,76},{16,80},{20,84},{24,88},{28,92},{32,9... | collective-permute-start | bytes 1179656 | tf_op jit(solution)/shard_map/ppermute | solution.py:11
  153.8 2.4 convert_reduce_fusion
  156.2 1.6 fusion.30
  157.7 3.8 %collective-permute-done.12 = bf16[8,16,2,768]{3,1,2,0:T(8,128)(2,1)S(1)} collective-permute-done((bf16[8,16,2,768]{3,1,2,0:T(8,128)(2,1)S(1)}, bf16[8,16,2,768]{3,1,2,0:T(8,128)(2,1)S(1)}, u32[]{:S(2)}, u32[]{:S(2)}) %collective-permute-start.12) | collective-permute-done | bytes 393248 | tf_op jit(solution)/shard_map/ppermute | solution.py:11
  161.8 5.4 %collective-permute-start.13 = (bf16[4,32,2,768]{3,1,2,0:T(8,128)(2,1)S(1)}, bf16[4,32,2,768]{3,1,2,0:T(8,128)(2,1)}, u32[]{:S(2)}, u32[]{:S(2)}) collective-permute-start(bf16[4,32,2,768]{3,1,2,0:T(8,128)(2,1)S(1)} %get-tuple-element.10), channel_id=1, source_target_pairs={{0,128},{4,132},{8,136},{12,140},{16,144},{20,148},{24,152},{28,15... | collective-permute-start | bytes 1179656 | tf_op jit(solution)/shard_map/ppermute | solution.py:11
  167.4 1.2 gather_fusion
  168.6 15.8 %collective-permute-done.13 = bf16[4,32,2,768]{3,1,2,0:T(8,128)(2,1)} collective-permute-done((bf16[4,32,2,768]{3,1,2,0:T(8,128)(2,1)S(1)}, bf16[4,32,2,768]{3,1,2,0:T(8,128)(2,1)}, u32[]{:S(2)}, u32[]{:S(2)}) %collective-permute-start.13) | collective-permute-done | bytes 393248 | tf_op jit(solution)/shard_map/ppermute | solution.py:11
  184.3 1.1 pad_maximum_fusion.4
  185.5 4.9 %collective-permute-start.14 = (bf16[2,64,2,768]{3,1,2,0:T(8,128)(2,1)S(1)}, bf16[2,64,2,768]{3,1,2,0:T(8,128)(2,1)S(1)}, u32[]{:S(2)}, u32[]{:S(2)}) collective-permute-start(bf16[2,64,2,768]{3,1,2,0:T(8,128)(2,1)S(1)} %get-tuple-element.8), channel_id=1, source_target_pairs={{0,256},{4,260},{8,264},{12,268},{16,272},{20,276},{24,280},{28,28... | collective-permute-start | bytes 1179656 | tf_op jit(solution)/shard_map/ppermute | solution.py:11
  191.3 3.5 %all-to-all-start.1 = ((bf16[4,64,768]{2,1,0:T(8,128)(2,1)}), bf16[4,64,768]{2,1,0:T(8,128)(2,1)S(1)}, u32[]{:S(2)}, u32[]{:S(2)}) async-start(bf16[4,64,768]{2,1,0:T(8,128)(2,1)} %broadcast_select_fusion.2), calls=%async_computation.1 | async-start | bytes 786432 | tf_op jit(solution)/shard_map/all_to_all | solution.py:58
  194.7 31.8 %collective-permute-done.14 = bf16[2,64,2,768]{3,1,2,0:T(8,128)(2,1)S(1)} collective-permute-done((bf16[2,64,2,768]{3,1,2,0:T(8,128)(2,1)S(1)}, bf16[2,64,2,768]{3,1,2,0:T(8,128)(2,1)S(1)}, u32[]{:S(2)}, u32[]{:S(2)}) %collective-permute-start.14) | collective-permute-done | bytes 393248 | tf_op jit(solution)/shard_map/ppermute | solution.py:11
  226.7 17.2 %collective-permute-start.15 = (bf16[1,128,2,768]{3,1,2,0:T(8,128)(2,1)S(1)}, bf16[1,128,2,768]{3,1,2,0:T(8,128)(2,1)S(1)}, u32[]{:S(2)}, u32[]{:S(2)}) collective-permute-start(bf16[1,128,2,768]{3,1,2,0:T(8,128)(2,1)S(1)} %get-tuple-element.6), channel_id=1, source_target_pairs={{0,512},{4,516},{8,520},{12,524},{16,528},{20,532},{24,536},{28,54... | collective-permute-start | bytes 1179656 | tf_op jit(solution)/shard_map/ppermute | solution.py:11
  244.3 14.8 %collective-permute-done.15 = bf16[1,128,2,768]{3,1,2,0:T(8,128)(2,1)S(1)} collective-permute-done((bf16[1,128,2,768]{3,1,2,0:T(8,128)(2,1)S(1)}, bf16[1,128,2,768]{3,1,2,0:T(8,128)(2,1)S(1)}, u32[]{:S(2)}, u32[]{:S(2)}) %collective-permute-start.15) | collective-permute-done | bytes 393248 | tf_op jit(solution)/shard_map/ppermute | solution.py:11
  260.3 1.2 gather_fusion.2
  261.6 2.2 multiply_reduce_fusion
  263.8 0.9 multiply_convert_fusion
  (92 shorter events, 10.8 us)
Async XLA Ops:
  0.0 261.6 %copy-start = (bf16[768,1024]{1,0:T(8,128)(2,1)S(1)}, bf16[768,1024]{1,0:T(8,128)(2,1)}, u32[]{:S(2)}) copy-start(bf16[768,1024]{1,0:T(8,128)(2,1)} %param.20) | copy-start | bytes 4718596
  0.0 71.6 %copy-start.1 = (bf16[512,768]{1,0:T(8,128)(2,1)S(1)}, bf16[512,768]{1,0:T(8,128)(2,1)}, u32[]{:S(2)}) copy-start(bf16[512,768]{1,0:T(8,128)(2,1)} %param.16) | copy-start | bytes 2359300
  3.6 17.0 %collective-permute-start = (s32[128,1,2]{2,0,1:T(8,128)S(1)}, s32[128,1,2]{2,0,1:T(8,128)S(1)}, u32[]{:S(2)}, u32[]{:S(2)}) collective-permute-start(s32[128,1,2]{2,0,1:T(8,128)S(1)} %bitcast.129), channel_id=1, source_target_pairs={{0,4},{4,0},{8,12},{12,8},{16,20},{20,16},{24,28},{28,24},{32,36},... | collective-permute-start | bytes 3080 | tf_op jit(solution)/shard_map/ppermute | solution.py:11
  20.7 4.3 %collective-permute-start.1 = (s32[64,2,2]{0,2,1:T(2,128)S(1)}, s32[64,2,2]{0,2,1:T(2,128)S(1)}, u32[]{:S(2)}, u32[]{:S(2)}) collective-permute-start(s32[64,2,2]{0,2,1:T(2,128)S(1)} %get-tuple-element.32), channel_id=1, source_target_pairs={{0,8},{4,12},{8,0},{12,4},{16,24},{20,28},{24,16},{28,20},{32,40},... | collective-permute-start | bytes 3080 | tf_op jit(solution)/shard_map/ppermute | solution.py:11
  25.4 5.3 %collective-permute-start.2 = (s32[32,4,2]{0,1,2:T(4,128)S(1)}, s32[32,4,2]{0,1,2:T(4,128)S(1)}, u32[]{:S(2)}, u32[]{:S(2)}) collective-permute-start(s32[32,4,2]{0,1,2:T(4,128)S(1)} %bitcast.138), channel_id=1, source_target_pairs={{0,16},{4,20},{8,24},{12,28},{16,0},{20,4},{24,8},{28,12},{32,48},... | collective-permute-start | bytes 3080 | tf_op jit(solution)/shard_map/ppermute | solution.py:11
  31.5 8.4 %collective-permute-start.3 = (s32[16,8,2]{1,2,0:T(2,128)S(1)}, s32[16,8,2]{1,2,0:T(2,128)S(1)}, u32[]{:S(2)}, u32[]{:S(2)}) collective-permute-start(s32[16,8,2]{1,2,0:T(2,128)S(1)} %get-tuple-element.24), channel_id=1, source_target_pairs={{0,32},{4,36},{8,40},{12,44},{16,48},{20,52},{24,56},{28,60},{32,0... | collective-permute-start | bytes 3080 | tf_op jit(solution)/shard_map/ppermute | solution.py:11
  40.0 4.4 %collective-permute-start.4 = (s32[8,16,2]{1,2,0:T(2,128)S(1)}, s32[8,16,2]{1,2,0:T(2,128)S(1)}, u32[]{:S(2)}, u32[]{:S(2)}) collective-permute-start(s32[8,16,2]{1,2,0:T(2,128)S(1)} %get-tuple-element.26), channel_id=1, source_target_pairs={{0,64},{4,68},{8,72},{12,76},{16,80},{20,84},{24,88},{28,92},{32,9... | collective-permute-start | bytes 3080 | tf_op jit(solution)/shard_map/ppermute | solution.py:11
  44.6 5.2 %collective-permute-start.5 = (s32[4,32,2]{1,2,0:T(2,128)S(1)}, s32[4,32,2]{1,2,0:T(2,128)S(1)}, u32[]{:S(2)}, u32[]{:S(2)}) collective-permute-start(s32[4,32,2]{1,2,0:T(2,128)S(1)} %get-tuple-element.28), channel_id=1, source_target_pairs={{0,128},{4,132},{8,136},{12,140},{16,144},{20,148},{24,152},{28,15... | collective-permute-start | bytes 3080 | tf_op jit(solution)/shard_map/ppermute | solution.py:11
  49.9 8.2 %collective-permute-start.6 = (s32[2,64,2]{1,2,0:T(2,128)S(1)}, s32[2,64,2]{1,2,0:T(2,128)S(1)}, u32[]{:S(2)}, u32[]{:S(2)}) collective-permute-start(s32[2,64,2]{1,2,0:T(2,128)S(1)} %get-tuple-element.30), channel_id=1, source_target_pairs={{0,256},{4,260},{8,264},{12,268},{16,272},{20,276},{24,280},{28,28... | collective-permute-start | bytes 3080 | tf_op jit(solution)/shard_map/ppermute | solution.py:11
  58.3 13.0 %collective-permute-start.7 = (s32[1,128,2]{1,2,0:T(2,128)S(1)}, s32[1,128,2]{1,2,0:T(2,128)S(1)}, u32[]{:S(2)}, u32[]{:S(2)}) collective-permute-start(s32[1,128,2]{1,2,0:T(2,128)S(1)} %get-tuple-element.34), channel_id=1, source_target_pairs={{0,512},{4,516},{8,520},{12,524},{16,528},{20,532},{24,536},{28,54... | collective-permute-start | bytes 3080 | tf_op jit(solution)/shard_map/ppermute | solution.py:11
  76.6 11.6 %collective-permute-start.8 = (bf16[128,1,2,768]{3,2,0,1:T(2,128)(2,1)S(1)}, bf16[128,1,2,768]{3,2,0,1:T(2,128)(2,1)S(1)}, u32[]{:S(2)}, u32[]{:S(2)}) collective-permute-start(bf16[128,1,2,768]{3,2,0,1:T(2,128)(2,1)S(1)} %get-tuple-element.18), channel_id=1, source_target_pairs={{0,4},{4,0},{8,12},{12,8},{16,20},{20,16},{24,28},{28,24},{32,36},... | collective-permute-start | bytes 1179656 | tf_op jit(solution)/shard_map/ppermute | solution.py:11
  89.4 12.2 %collective-permute-start.9 = (bf16[64,2,2,768]{3,2,0,1:T(2,128)(2,1)S(1)}, bf16[64,2,2,768]{3,2,0,1:T(2,128)(2,1)S(1)}, u32[]{:S(2)}, u32[]{:S(2)}) collective-permute-start(bf16[64,2,2,768]{3,2,0,1:T(2,128)(2,1)S(1)} %get-tuple-element.16), channel_id=1, source_target_pairs={{0,8},{4,12},{8,0},{12,4},{16,24},{20,28},{24,16},{28,20},{32,40},... | collective-permute-start | bytes 1179656 | tf_op jit(solution)/shard_map/ppermute | solution.py:11
  103.5 22.2 %collective-permute-start.10 = (bf16[32,4,2,768]{3,2,1,0:T(2,128)(2,1)S(1)}, bf16[32,4,2,768]{3,2,1,0:T(2,128)(2,1)S(1)}, u32[]{:S(2)}, u32[]{:S(2)}) collective-permute-start(bf16[32,4,2,768]{3,2,1,0:T(2,128)(2,1)S(1)} %slice_bitcast_fusion.9), channel_id=1, source_target_pairs={{0,16},{4,20},{8,24},{12,28},{16,0},{20,4},{24,8},{28,12},{32,48},... | collective-permute-start | bytes 1179656 | tf_op jit(solution)/shard_map/ppermute | solution.py:11
  127.5 21.5 %collective-permute-start.11 = (bf16[16,8,2,768]{3,2,1,0:T(2,128)(2,1)S(1)}, bf16[16,8,2,768]{3,2,1,0:T(2,128)(2,1)S(1)}, u32[]{:S(2)}, u32[]{:S(2)}) collective-permute-start(bf16[16,8,2,768]{3,2,1,0:T(2,128)(2,1)S(1)} %get-tuple-element.14), channel_id=1, source_target_pairs={{0,32},{4,36},{8,40},{12,44},{16,48},{20,52},{24,56},{28,60},{32,0... | collective-permute-start | bytes 1179656 | tf_op jit(solution)/shard_map/ppermute | solution.py:11
  129.5 37.8 %all-to-all-start = ((s32[4,1,64]{2,1,0:T(1,128)}), s32[4,1,64]{2,1,0:T(1,128)S(1)}, u32[]{:S(2)}, u32[]{:S(2)}) async-start(s32[4,1,64]{2,1,0:T(1,128)} %bitcast.1), calls=%async_computation | async-start | bytes 4096 | tf_op jit(solution)/shard_map/all_to_all | solution.py:55
  150.2 3.6 %copy-start.5 = (s32[256,25]{0,1:T(8,128)S(1)}, s32[256,25]{0,1:T(8,128)}, u32[]{:S(2)}) copy-start(s32[256,25]{0,1:T(8,128)} %param.12) | copy-start | bytes 76804
  150.2 6.0 %copy-start.3 = (bf16[768,1024]{1,0:T(8,128)(2,1)S(1)}, bf16[768,1024]{1,0:T(8,128)(2,1)}, u32[]{:S(2)}) copy-start(bf16[768,1024]{1,0:T(8,128)(2,1)} %param.19) | copy-start | bytes 4718596
  150.2 6.0 %copy-start.4 = (bf16[256,768]{1,0:T(8,128)(2,1)S(1)}, bf16[256,768]{1,0:T(8,128)(2,1)}, u32[]{:S(2)}) copy-start(bf16[256,768]{1,0:T(8,128)(2,1)} %param.11) | copy-start | bytes 1179652
  150.4 11.2 %collective-permute-start.12 = (bf16[8,16,2,768]{3,1,2,0:T(8,128)(2,1)S(1)}, bf16[8,16,2,768]{3,1,2,0:T(8,128)(2,1)S(1)}, u32[]{:S(2)}, u32[]{:S(2)}) collective-permute-start(bf16[8,16,2,768]{3,1,2,0:T(8,128)(2,1)S(1)} %get-tuple-element.12), channel_id=1, source_target_pairs={{0,64},{4,68},{8,72},{12,76},{16,80},{20,84},{24,88},{28,92},{32,9... | collective-permute-start | bytes 1179656 | tf_op jit(solution)/shard_map/ppermute | solution.py:11
  161.6 5.6 %copy-start.6 = (s32[1,1,256]{2,1,0:T(1,128)S(1)}, s32[1,1,256]{2,1,0:T(1,128)}, u32[]{:S(2)}) copy-start(s32[1,1,256]{2,1,0:T(1,128)} %param.17) | copy-start | bytes 3076
  161.6 5.7 %copy-start.2 = (bf16[512,768]{1,0:T(8,128)(2,1)S(1)}, bf16[512,768]{1,0:T(8,128)(2,1)}, u32[]{:S(2)}) copy-start(bf16[512,768]{1,0:T(8,128)(2,1)} %param.13) | copy-start | bytes 2359300
  161.8 22.5 %collective-permute-start.13 = (bf16[4,32,2,768]{3,1,2,0:T(8,128)(2,1)S(1)}, bf16[4,32,2,768]{3,1,2,0:T(8,128)(2,1)}, u32[]{:S(2)}, u32[]{:S(2)}) collective-permute-start(bf16[4,32,2,768]{3,1,2,0:T(8,128)(2,1)S(1)} %get-tuple-element.10), channel_id=1, source_target_pairs={{0,128},{4,132},{8,136},{12,140},{16,144},{20,148},{24,152},{28,15... | collective-permute-start | bytes 1179656 | tf_op jit(solution)/shard_map/ppermute | solution.py:11
  185.5 41.0 %collective-permute-start.14 = (bf16[2,64,2,768]{3,1,2,0:T(8,128)(2,1)S(1)}, bf16[2,64,2,768]{3,1,2,0:T(8,128)(2,1)S(1)}, u32[]{:S(2)}, u32[]{:S(2)}) collective-permute-start(bf16[2,64,2,768]{3,1,2,0:T(8,128)(2,1)S(1)} %get-tuple-element.8), channel_id=1, source_target_pairs={{0,256},{4,260},{8,264},{12,268},{16,272},{20,276},{24,280},{28,28... | collective-permute-start | bytes 1179656 | tf_op jit(solution)/shard_map/ppermute | solution.py:11
  191.3 52.9 %all-to-all-start.1 = ((bf16[4,64,768]{2,1,0:T(8,128)(2,1)}), bf16[4,64,768]{2,1,0:T(8,128)(2,1)S(1)}, u32[]{:S(2)}, u32[]{:S(2)}) async-start(bf16[4,64,768]{2,1,0:T(8,128)(2,1)} %broadcast_select_fusion.2), calls=%async_computation.1 | async-start | bytes 786432 | tf_op jit(solution)/shard_map/all_to_all | solution.py:58
  226.6 17.4 %copy-start.8 = (s32[1,1,4]{2,1,0:T(1,128)S(1)}, s32[1,1,4]{2,1,0:T(1,128)}, u32[]{:S(2)}) copy-start(s32[1,1,4]{2,1,0:T(1,128)} %param.15) | copy-start | bytes 52
  226.7 32.3 %collective-permute-start.15 = (bf16[1,128,2,768]{3,1,2,0:T(8,128)(2,1)S(1)}, bf16[1,128,2,768]{3,1,2,0:T(8,128)(2,1)S(1)}, u32[]{:S(2)}, u32[]{:S(2)}) collective-permute-start(bf16[1,128,2,768]{3,1,2,0:T(8,128)(2,1)S(1)} %get-tuple-element.6), channel_id=1, source_target_pairs={{0,512},{4,516},{8,520},{12,524},{16,528},{20,532},{24,536},{28,54... | collective-permute-start | bytes 1179656 | tf_op jit(solution)/shard_map/ppermute | solution.py:11
  260.3 1.3 copy-start.7
where the time goes:
time: 270 us; the launch traced here: 265 us
  waiting for transfers between devices  146 us (54%)
  starting transfers between devices  88.2 us (33%)
  local copies, waits for them, and re-layouts  13.9 us (5%)
  other arithmetic  12.7 us (5%)
  matrix products  3.77 us (1%)
    ppermute x16, waiting for transfers between devices, from_partner(): lax.ppermute(array, axis, [(i, i ^ 1 << distance) for i in range(lax.axis...  146 us
    ppermute x16, starting transfers between devices, from_partner(): lax.ppermute(array, axis, [(i, i ^ 1 << distance) for i in range(lax.axis...  81.2 us
  transfers between devices with their start and end apart: 18, of which 16 were waited for; matrix products, arithmetic and copies ran while one was open for 3% of the time, Pallas kernels for 0%

commit v1 on v0

--- a/solution.py
+++ b/solution.py
@@ -7,28 +7,8 @@
 CCAP = 2
 
 
-def from_partner(array, axis, distance):
-    return lax.ppermute(array, axis, [(i, i ^ 1 << distance) for i in range(lax.axis_size(axis))])
-
-
-def relay(buffer, mover):
-    groups = buffer.shape[0]
-    depth = groups.bit_length() - 1
-    levels = list(range(depth))
-    tail = buffer.shape[1:]
-    for bit_index in levels:
-        shaped = buffer.reshape((groups >> bit_index + 1, 2, 1 << bit_index) + tail)
-        arrived = mover(shaped[:, 1], bit_index)
-        buffer = jnp.stack([shaped[:, 0], arrived], axis=1).reshape(buffer.shape)
-    return buffer
-
-
-def move_ids(buffer, bit_index):
-    return from_partner(buffer, "group", bit_index)
-
-
-def move_rows(buffer, bit_index):
-    return from_partner(buffer, "group", bit_index)
+def exchange(buffer):
+    return lax.all_to_all(buffer, "group", split_axis=0, concat_axis=0, tiled=True)
 
 
 def per_device(
@@ -48,7 +28,6 @@
     hot_slots = hot_req.shape[3]
     width = hot_table.shape[1]
     groups = lax.axis_size("group")
-    myself = lax.axis_index("group")
     asked_hot = hot_req.reshape(members, hot_slots)
     rows_out = jnp.take(
         hot_table,
@@ -67,12 +46,11 @@
     same_owner = owners[:, None] == owners[None, :]
     earlier = position[:, None] > position[None, :]
     rank = jnp.sum((same_owner & earlier).astype(jnp.int32), axis=1)
-    relative = jnp.bitwise_xor(owners, myself)
-    flat_slot = relative * CCAP + rank
+    flat_slot = owners * CCAP + rank
     id_buffer = jnp.zeros((groups * CCAP,), jnp.int32).at[flat_slot].set(wanted)
-    asked_cold = relay(id_buffer.reshape(groups, CCAP), move_ids)
+    asked_cold = exchange(id_buffer.reshape(groups, CCAP))
     served = jnp.take(cold_table, asked_cold.reshape(-1), axis=0).reshape(groups, CCAP, width)
-    returned = relay(served, move_rows)
+    returned = exchange(served)
     cold_rows = jnp.take(returned.reshape(groups * CCAP, width), flat_slot, axis=0)
     self_part = jnp.dot(targets, w_self, preferred_element_type=jnp.float32)
     fetched = jnp.concatenate([hot_rows, cold_rows], axis=0)

time: 270 us -> 130 us (0.48); the launches traced: 265 us -> 129 us
  waiting for transfers between devices: 146 us -> 56.6 us
  starting transfers between devices: 88.2 us -> 46.7 us
  local copies, waits for them, and re-layouts: 13.9 us -> 9.67 us
    ppermute x16 -> x0, waiting for transfers between devices: 146 us -> none  [from_partner(): lax.ppermute(array, axis, [(i, i ^ 1 << distance) for i in range(lax.axis...]
    ppermute x16 -> x0, starting transfers between devices: 81.2 us -> none  [from_partner(): lax.ppermute(array, axis, [(i, i ^ 1 << distance) for i in range(lax.axis...]
    all_to_all x0 -> x2, waiting for transfers between devices: none -> 56.5 us  [exchange(): lax.all_to_all(buffer, 'group', split_axis=0, concat_axis=0, tiled=True)]
    all_to_all x0 -> x2, starting transfers between devices: none -> 38.3 us  [exchange(): lax.all_to_all(buffer, 'group', split_axis=0, concat_axis=0, tiled=True)]
    another operation x27 -> x0, local copies, waits for them, and re-layouts: 4.59 us -> none  [the longest x17 3.18 us: relay(): buffer = jnp.stack([shaped[:, 0], arrived], axis=1).reshape(buffer.shape)]
    another operation x15 -> x0, other arithmetic: 4.33 us -> none  [relay(): buffer = jnp.stack([shaped[:, 0], arrived], axis=1).reshape(buffer.shape)]
  transfers between devices with their start and end apart: 18 -> 4, of which waited for: 16 -> 3; matrix products, arithmetic and copies ran while one was open for 3% -> 16% of each run, Pallas kernels for 0% -> 0%
where the time goes in v1:
time: 130 us; the launch traced here: 129 us
  waiting for transfers between devices  56.6 us (44%)
  starting transfers between devices  46.7 us (36%)
  other arithmetic  10.9 us (8%)
  local copies, waits for them, and re-layouts  9.67 us (7%)
  matrix products  5.16 us (4%)
    all_to_all x2, waiting for transfers between devices, exchange(): lax.all_to_all(buffer, 'group', split_axis=0, concat_axis=0, tiled=True)  56.5 us
    all_to_all x2, starting transfers between devices, exchange(): lax.all_to_all(buffer, 'group', split_axis=0, concat_axis=0, tiled=True)  38.3 us
    all_to_all x1, starting transfers between devices, per_device(): lax.all_to_all(asked_hot, 'member', split_axis=0, concat_axis=0, tiled=True)  4.97 us
    all_to_all x1, starting transfers between devices, per_device(): lax.all_to_all(rows_out, 'member', split_axis=0, concat_axis=0, tiled=True)  3.46 us
    dot_general x1, matrix products, per_device(): self_part = jnp.dot(targets, w_self, preferred_element_type=jnp.float32)  2.95 us
    gather x1, local copies, waits for them, and re-layouts, per_device(): jnp.take(hot_table, lax.all_to_all(asked_hot, 'member', split_axis=0, con...  2.63 us
  transfers between devices with their start and end apart: 4, of which 3 were waited for; matrix products, arithmetic and copies ran while one was open for 16% of the time, Pallas kernels for 0%

profile of v1, /device:TPU:1, one launch (start us, length us, event | category | flops | bytes accessed | tf_op | source)
XLA Modules:
  0.0 129.3 jit_solution(17138673621041134971)
XLA Ops:
  0.0 0.0 copy-start
  0.0 5.0 %all-to-all-start = ((s32[4,1,64]{2,1,0:T(1,128)}), s32[4,1,64]{2,1,0:T(1,128)S(1)}, u32[]{:S(2)}, u32[]{:S(2)}) async-start(s32[4,1,64]{2,1,0:T(1,128)} %bitcast.34), calls=%async_computation | async-start | bytes 4096 | tf_op jit(solution)/shard_map/all_to_all | solution.py:34
  5.0 0.9 convert_reduce_fusion.1
  5.9 0.7 compare_select_fusion.2
  6.6 1.6 %scatter_custom_fusion = s32[512]{0:T(512)S(1)} fusion(s32[256]{0:T(256)S(1)} %bitcast.32, s32[256]{0:T(256)} %bitcast.35, s32[]{:T(128)} %constant.27.clone.1), kind=kCustom, calls=%fused_computation.40 | custom fusion | bytes 2560 | tf_op jit(solution)/shard_map/scatter | solution.py:50
  8.2 0.8 all_to_all.27
  8.9 0.1 all-to-all-done
  9.0 29.0 %all-to-all-start.2 = ((s32[256,1,2]{2,1,0:T(1,128)}), s32[256,1,2]{2,1,0:T(1,128)S(1)}, u32[]{:S(2)}, u32[]{:S(2)}) async-start(s32[256,1,2]{2,1,0:T(1,128)} %bitcast.11), calls=%async_computation.2 | async-start | bytes 262144 | tf_op jit(solution)/shard_map/all_to_all | solution.py:11
  38.0 0.1 reshape.173
  38.1 2.6 %gather_fusion = bf16[256,768]{1,0:T(8,128)(2,1)S(1)} fusion(bf16[512,768]{1,0:T(8,128)(2,1)} %param.13, s32[1024]{0:T(1024)S(1)} %pad_clamp_fusion.2), kind=kCustom, calls=%fused_computation | custom fusion | bytes 787456 | tf_op jit(solution)/shard_map/jit(_take)/gather | solution.py:32
  40.7 0.0 copy-start.1
  40.7 0.9 broadcast_select_fusion.2
  41.6 15.8 %all-to-all-done.2 = s32[256,1,2]{2,1,0:T(1,128)S(1)} async-done(((s32[256,1,2]{2,1,0:T(1,128)}), s32[256,1,2]{2,1,0:T(1,128)S(1)}, u32[]{:S(2)}, u32[]{:S(2)}) %all-to-all-start.2) | async-done | bytes 2080 | tf_op jit(solution)/shard_map/all_to_all | solution.py:11
  57.4 3.5 %all-to-all-start.1 = ((bf16[4,64,768]{2,1,0:T(8,128)(2,1)}), bf16[4,64,768]{2,1,0:T(8,128)(2,1)S(1)}, u32[]{:S(2)}, u32[]{:S(2)}) async-start(bf16[4,64,768]{2,1,0:T(8,128)(2,1)} %broadcast_select_fusion.2), calls=%async_computation.1 | async-start | bytes 786432 | tf_op jit(solution)/shard_map/all_to_all | solution.py:37
  60.9 0.5 broadcast.123
  61.4 0.9 reduce.3
  62.3 0.1 reshape.169
  62.5 0.6 compare_and_fusion
  63.1 0.0 copy-done.1
  63.2 2.0 %gather_fusion.1 = bf16[512,768]{1,0:T(8,128)(2,1)S(1)} fusion(bf16[512,768]{1,0:T(8,128)(2,1)S(1)} %copy-done.1, s32[1024]{0:T(1024)S(1)} %pad_clamp_fusion.1), kind=kCustom, calls=%fused_computation.1 | custom fusion | bytes 1574912 | tf_op jit(solution)/shard_map/jit(_take)/gather | solution.py:52
  65.2 0.3 gather.16
  65.5 0.0 copy-start.7
  65.5 0.0 copy-start.5
  65.5 0.0 copy-start.4
  65.5 0.0 copy-start.3
  65.5 2.5 %broadcast_select_fusion = bf16[256,2,768]{2,1,0:T(2,128)(2,1)} fusion(bf16[256,2,768]{2,1,0:T(2,128)(2,1)S(1)} %gather.16, pred[256,2]{1,0:T(8,128)(4,1)} %compare_and_fusion), kind=kLoop, calls=%fused_computation.6 | loop fusion | flops 393216 | bytes 1573376 | tf_op jit(solution)/shard_map/jit(_take)/select_n | solution.py:52
  68.0 0.0 all-to-all-done.1
  68.0 9.3 %all-to-all-start.3 = ((bf16[256,2,768]{2,1,0:T(2,128)(2,1)}), bf16[256,2,768]{2,1,0:T(2,128)(2,1)S(1)}, u32[]{:S(2)}, u32[]{:S(2)}) async-start(bf16[256,2,768]{2,1,0:T(2,128)(2,1)} %broadcast_select_fusion), calls=%async_computation.3 | async-start | bytes 1572864 | tf_op jit(solution)/shard_map/all_to_all | solution.py:11
  77.3 0.0 copy-done.7
  77.3 0.1 iota_compare_fusion.2
  77.4 0.1 lt.88
  77.5 0.0 copy-done.5
  77.5 0.0 copy-done.4
  77.5 2.4 %convert_reduce_fusion = bf16[256,512]{1,0:T(8,128)(2,1)} fusion(s32[256,25]{0,1:T(8,128)S(1)} %copy-done.4), kind=kLoop, calls=%fused_computation.4 | loop fusion | flops 9699328 | bytes 287744 | tf_op jit(solution)/shard_map/reduce_sum | solution.py:58
  79.9 0.0 copy-done.3
  79.9 3.0 %fusion.20 = f32[256,1024]{1,0:T(8,128)} fusion(bf16[256,768]{1,0:T(8,128)(2,1)S(1)} %copy-done.3, bf16[768,1024]{1,0:T(8,128)(2,1)} %param.19), kind=kOutput, calls=%fused_computation.44 | convolution fusion | flops 402653184 | bytes 3014656 | tf_op jit(solution)/shard_map/dot_general | solution.py:55
  82.9 0.9 bitcast_select_fusion
  83.7 40.7 %all-to-all-done.3 = bf16[256,2,768]{2,1,0:T(2,128)(2,1)S(1)} async-done(((bf16[256,2,768]{2,1,0:T(2,128)(2,1)}), bf16[256,2,768]{2,1,0:T(2,128)(2,1)S(1)}, u32[]{:S(2)}, u32[]{:S(2)}) %all-to-all-start.3) | async-done | bytes 786464 | tf_op jit(solution)/shard_map/all_to_all | solution.py:11
  124.5 0.3 reshape.170
  124.8 0.0 copy-start.2
  124.8 0.0 copy-start.6
  124.8 1.2 gather_fusion.2
  126.0 0.1 broadcast_select_fusion.1
  126.1 0.0 copy-done
  126.1 0.0 copy-done.2
  126.1 0.0 copy-done.6
  126.1 2.2 %multiply_reduce_fusion = (f32[256]{0:T(256)S(1)}, f32[256,1024]{1,0:T(8,128)S(1)}) fusion(f32[1024]{0:T(1024)S(1)} %copy-done.6, f32[256,1024]{1,0:T(8,128)} %fusion.20, bf16[768,1024]{1,0:T(8,128)(2,1)S(1)} %copy-done, bf16[256,768]{1,0:T(8,128)(2,1)S(1)} %broadcast_select_fusion.1, bf16[256,768]{1,0:T(8,128)(2,1)S(1)} %copy-done.2, ...), kind=kOutput, calls=%fused_computation.13 | convolution fusion | flops 607256320 | bytes 4723712 | tf_op jit(solution)/shard_map/dot_general | solution.py:61
  128.3 0.9 multiply_convert_fusion
  (8 shorter events, 0.1 us)
Async XLA Ops:
  0.0 126.1 %copy-start = (bf16[768,1024]{1,0:T(8,128)(2,1)S(1)}, bf16[768,1024]{1,0:T(8,128)(2,1)}, u32[]{:S(2)}) copy-start(bf16[768,1024]{1,0:T(8,128)(2,1)} %param.20) | copy-start | bytes 4718596
  0.0 9.0 %all-to-all-start = ((s32[4,1,64]{2,1,0:T(1,128)}), s32[4,1,64]{2,1,0:T(1,128)S(1)}, u32[]{:S(2)}, u32[]{:S(2)}) async-start(s32[4,1,64]{2,1,0:T(1,128)} %bitcast.34), calls=%async_computation | async-start | bytes 4096 | tf_op jit(solution)/shard_map/all_to_all | solution.py:34
  9.0 48.4 %all-to-all-start.2 = ((s32[256,1,2]{2,1,0:T(1,128)}), s32[256,1,2]{2,1,0:T(1,128)S(1)}, u32[]{:S(2)}, u32[]{:S(2)}) async-start(s32[256,1,2]{2,1,0:T(1,128)} %bitcast.11), calls=%async_computation.2 | async-start | bytes 262144 | tf_op jit(solution)/shard_map/all_to_all | solution.py:11
  40.7 22.4 %copy-start.1 = (bf16[512,768]{1,0:T(8,128)(2,1)S(1)}, bf16[512,768]{1,0:T(8,128)(2,1)}, u32[]{:S(2)}) copy-start(bf16[512,768]{1,0:T(8,128)(2,1)} %param.16) | copy-start | bytes 2359300
  57.4 10.6 %all-to-all-start.1 = ((bf16[4,64,768]{2,1,0:T(8,128)(2,1)}), bf16[4,64,768]{2,1,0:T(8,128)(2,1)S(1)}, u32[]{:S(2)}, u32[]{:S(2)}) async-start(bf16[4,64,768]{2,1,0:T(8,128)(2,1)} %broadcast_select_fusion.2), calls=%async_computation.1 | async-start | bytes 786432 | tf_op jit(solution)/shard_map/all_to_all | solution.py:37
  65.5 11.8 %copy-start.7 = (s32[1,1,4]{2,1,0:T(1,128)S(1)}, s32[1,1,4]{2,1,0:T(1,128)}, u32[]{:S(2)}) copy-start(s32[1,1,4]{2,1,0:T(1,128)} %param.15) | copy-start | bytes 52
  65.5 12.0 %copy-start.5 = (s32[1,1,256]{2,1,0:T(1,128)S(1)}, s32[1,1,256]{2,1,0:T(1,128)}, u32[]{:S(2)}) copy-start(s32[1,1,256]{2,1,0:T(1,128)} %param.17) | copy-start | bytes 3076
  65.5 12.0 %copy-start.4 = (s32[256,25]{0,1:T(8,128)S(1)}, s32[256,25]{0,1:T(8,128)}, u32[]{:S(2)}) copy-start(s32[256,25]{0,1:T(8,128)} %param.12) | copy-start | bytes 76804
  65.5 14.4 %copy-start.3 = (bf16[256,768]{1,0:T(8,128)(2,1)S(1)}, bf16[256,768]{1,0:T(8,128)(2,1)}, u32[]{:S(2)}) copy-start(bf16[256,768]{1,0:T(8,128)(2,1)} %param.11) | copy-start | bytes 1179652
  68.0 56.4 %all-to-all-start.3 = ((bf16[256,2,768]{2,1,0:T(2,128)(2,1)}), bf16[256,2,768]{2,1,0:T(2,128)(2,1)S(1)}, u32[]{:S(2)}, u32[]{:S(2)}) async-start(bf16[256,2,768]{2,1,0:T(2,128)(2,1)} %broadcast_select_fusion), calls=%async_computation.3 | async-start | bytes 1572864 | tf_op jit(solution)/shard_map/all_to_all | solution.py:11
  124.8 1.3 %copy-start.2 = (bf16[256,768]{1,0:T(8,128)(2,1)S(1)}, bf16[256,768]{1,0:T(8,128)(2,1)}, u32[]{:S(2)}) copy-start(bf16[256,768]{1,0:T(8,128)(2,1)} %bitcast_select_fusion) | copy-start | bytes 1179652
  124.8 1.3 %copy-start.6 = (f32[1024]{0:T(1024)S(1)}, f32[1024]{0:T(1024)}, u32[]{:S(2)}) copy-start(f32[1024]{0:T(1024)} %param.21) | copy-start | bytes 12292

commit v2 on v1

v2 whole, which is shorter than its diff:
```python
import functools

import jax
import jax.numpy as jnp
from jax import lax
from jax.experimental import pallas as pl
from jax.experimental.pallas import tpu as pltpu
from jax.sharding import PartitionSpec as P

FANOUT = 25
LANES = 128
CHUNKS = 3
MESH = pl.DeviceIdType.MESH


def wait_bytes(ref, sem):
    pltpu.make_async_copy(ref, ref, sem).wait()


def one_hot(index, width):
    columns = lax.broadcasted_iota(jnp.int32, (index.shape[0], width), 1)
    return (columns == index).astype(jnp.float32).astype(jnp.bfloat16)


def lane_to_rows(row, rows, first):
    wide = jnp.broadcast_to(row, (rows, LANES))
    lane = lax.broadcasted_iota(jnp.int32, (rows, LANES), 1)
    slot = lax.broadcasted_iota(jnp.int32, (rows, LANES), 0)
    return jnp.sum(jnp.where(lane == slot + first, wide, 0), axis=1, keepdims=True)


def exact_dot(a, b):
    return jnp.dot(a, b, preferred_element_type=jnp.float32)


def exchange_kernel(
    nz,
    nyc,
    nm,
    ask_ref,
    hot_ask_ref,
    table_ref,
    hot_ref,
    cold_ref,
    extra_ref,
    hot_rows_ref,
    ids_a,
    ids_b,
    ids_c,
    hot_ids,
    square,
    hits,
    hits_x,
    z_out,
    z_in,
    y_out,
    y_in,
    x_out,
    x_in,
    row_out,
    row_in,
    h_out,
    h_in,
    send_ids,
    recv_ids,
    send_z,
    recv_z,
    send_y,
    recv_y,
    send_x,
    recv_x,
    send_h,
    recv_h,
):
    group, member = lax.axis_index("group"), lax.axis_index("member")
    z, yc = group // nyc, group % nyc
    ngroup = nz * nyc
    width = table_ref.shape[1] // CHUNKS
    owned = table_ref.shape[0]
    slots = h_out.shape[0] // nm

    def z_peer(step):
        far = nz // 2 - (step + 1) // 2
        return (z + nz + (1 - 2 * (step % 2)) * far) % nz

    def yc_peer(step):
        return (yc + 1 + step) % nyc

    def m_peer(step):
        return (member + 1 + step) % nm

    def to_z(peer):
        return (peer * nyc + yc, member)

    def to_yc(peer):
        return (z * nyc + peer, member)

    def to_m(peer):
        return (group, peer)

    def each(count, body):
        lax.fori_loop(0, count, lambda i, c: (body(i), c)[1], 0)

    def send(source, target, send_sem, recv_sem, device):
        pltpu.make_async_remote_copy(
            src_ref=source, dst_ref=target, send_sem=send_sem, recv_sem=recv_sem, device_id=device, device_id_type=MESH
        ).start()

    def block(peer, rows):
        return pl.ds(pl.multiple_of(peer * rows, rows), rows)

    barrier = pltpu.get_barrier_semaphore()

    def greet(device):
        pl.semaphore_signal(barrier, inc=1, device_id=device, device_id_type=MESH)

    each(nz - 1, lambda i: greet(to_z(z_peer(i))))
    each(nyc - 1, lambda i: greet(to_yc(yc_peer(i))))
    each(nm - 1, lambda i: greet(to_m(m_peer(i))))
    pl.semaphore_wait(barrier, nz + nyc + nm - 3)

    def send_ids_yc(i):
        peer = yc_peer(i)
        send(ask_ref.at[peer], ids_a.at[yc], send_ids.at[0], recv_ids.at[0], to_yc(peer))

    each(nyc - 1, send_ids_yc)

    def send_ids_m(i):
        peer = m_peer(i)
        send(hot_ask_ref.at[peer], hot_ids.at[member], send_ids.at[2], recv_ids.at[2], to_m(peer))

    each(nm - 1, send_ids_m)
    ids_a[yc] = ask_ref[yc]
    hot_ids[member] = hot_ask_ref[member]
    square[...] = jnp.zeros_like(square)

    wait_bytes(ids_a.at[pl.ds(0, nyc - 1)], recv_ids.at[0])
    for peer in range(nyc):
        square[peer : peer + 1, :] = ids_a[peer, 0:1, :]
        square[nyc + peer : nyc + peer + 1, :] = ids_a[peer, 1:2, :]
    square[...] = square[...].T
    for peer in range(nz):
        ids_b[peer] = square[peer : peer + 1, :]

    def send_ids_z(i):
        peer = z_peer(i)
        send(ids_b.at[peer], ids_c.at[z], send_ids.at[1], recv_ids.at[1], to_z(peer))

    each(nz - 1, send_ids_z)
    ids_c[z] = ids_b[z]

    wait_bytes(hot_ids.at[pl.ds(0, nm - 1)], recv_ids.at[2])
    for peer in range(nm):
        wanted = one_hot(lane_to_rows(hot_ids[peer], slots, 0), hot_ref.shape[0])
        h_out[peer * slots : (peer + 1) * slots, :] = exact_dot(wanted, hot_ref[...]).astype(jnp.bfloat16)

    def send_hot(i):
        peer = m_peer(i)
        send(h_out.at[block(peer, slots)], h_in.at[block(member, slots)], send_h, recv_h, to_m(peer))

    each(nm - 1, send_hot)
    h_in[block(member, slots), :] = h_out[block(member, slots), :]

    rows_to = lax.broadcasted_iota(jnp.int32, (ngroup, ngroup), 0)
    rows_from = lax.broadcasted_iota(jnp.int32, (ngroup, ngroup), 1)
    turn = (rows_from == lax.rem(rows_to, nz) * nyc + lax.div(rows_to, nz)).astype(jnp.float32).astype(jnp.bfloat16)

    wait_bytes(ids_c.at[pl.ds(0, nz - 1)], recv_ids.at[1])
    for peer in range(nz):
        hits[peer * nyc : (peer + 1) * nyc, :] = one_hot(lane_to_rows(ids_c[peer], nyc, 0), owned)
        hits_x[peer * nyc : (peer + 1) * nyc, :] = one_hot(lane_to_rows(ids_c[peer], nyc, nyc), owned)

    def gather_and_send(chunk):
        z_out[chunk] = exact_dot(hits[...], table_ref[:, chunk * width : (chunk + 1) * width]).astype(jnp.bfloat16)

        def send_rows(i):
            peer = z_peer(i)
            send(
                z_out.at[chunk, block(peer, nyc)],
                z_in.at[chunk, block(z, nyc)],
                send_z.at[chunk],
                recv_z.at[chunk],
                to_z(peer),
            )

        each(nz - 1, send_rows)
        z_in[chunk, block(z, nyc), :] = z_out[chunk, block(z, nyc), :]

    gather_and_send(0)

    ordered = exact_dot(turn, hits_x[...]).astype(jnp.bfloat16)
    x_out[...] = exact_dot(ordered, table_ref[...]).astype(jnp.bfloat16)

    def send_extra(i):
        peer = yc_peer(i)
        send(x_out.at[block(peer, nz)], x_in.at[block(yc, nz)], send_x.at[0], recv_x.at[0], to_yc(peer))

    each(nyc - 1, send_extra)
    x_in[block(yc, nz), :] = x_out[block(yc, nz), :]

    for chunk in range(1, CHUNKS):
        gather_and_send(chunk)

    def turn_and_send(chunk):
        wait_bytes(z_in.at[chunk, pl.ds(0, (nz - 1) * nyc)], recv_z.at[chunk])
        y_out[chunk] = exact_dot(turn, z_in[chunk]).astype(jnp.bfloat16)

        def send_rows(i):
            peer = yc_peer(i)
            send(
                y_out.at[chunk, block(peer, nz)],
                y_in.at[chunk, block(yc, nz)],
                send_y.at[chunk],
                recv_y.at[chunk],
                to_yc(peer),
            )

        each(nyc - 1, send_rows)
        y_in[chunk, block(yc, nz), :] = y_out[chunk, block(yc, nz), :]

    turn_and_send(0)

    wait_bytes(x_in.at[pl.ds(0, (nyc - 1) * nz)], recv_x.at[0])
    target = lax.broadcasted_iota(jnp.int32, (nz, ngroup), 0)
    source = lax.broadcasted_iota(jnp.int32, (nz, ngroup), 1)
    pick = (lax.rem(source, nz) == target).astype(jnp.float32).astype(jnp.bfloat16)
    picked = exact_dot(pick, x_in[...])
    for peer in range(nz):
        row_out[peer] = picked[peer : peer + 1, :]

    def send_extra_row(i):
        peer = z_peer(i)
        send(row_out.at[peer], row_in.at[z], send_x.at[1], recv_x.at[1], to_z(peer))

    each(nz - 1, send_extra_row)
    row_in[z] = row_out[z]

    for chunk in range(1, CHUNKS):
        turn_and_send(chunk)

    wait_bytes(h_in.at[pl.ds(0, (nm - 1) * slots)], recv_h)
    hot_rows_ref[...] = h_in[...]
    wait_bytes(row_in.at[pl.ds(0, nz - 1)], recv_x.at[1])
    extra = row_in[0]
    for peer in range(1, nz):
        extra = extra + row_in[peer]
    extra_ref[...] = extra
    for chunk in range(CHUNKS):
        wait_bytes(y_in.at[chunk, pl.ds(0, (nyc - 1) * nz)], recv_y.at[chunk])
        cold_ref[:, chunk * width : (chunk + 1) * width] = y_in[chunk]

    wait_bytes(ids_a.at[pl.ds(0, nyc - 1)], send_ids.at[0])
    wait_bytes(ids_c.at[pl.ds(0, nz - 1)], send_ids.at[1])
    wait_bytes(hot_ids.at[pl.ds(0, nm - 1)], send_ids.at[2])
    wait_bytes(h_in.at[pl.ds(0, (nm - 1) * slots)], send_h)
    wait_bytes(x_in.at[pl.ds(0, (nyc - 1) * nz)], send_x.at[0])
    wait_bytes(row_in.at[pl.ds(0, nz - 1)], send_x.at[1])
    for chunk in range(CHUNKS):
        wait_bytes(z_in.at[chunk, pl.ds(0, (nz - 1) * nyc)], send_z.at[chunk])
        wait_bytes(y_in.at[chunk, pl.ds(0, (nyc - 1) * nz)], send_y.at[chunk])


def exchange(nz, nyc, nm, ask, hot_ask, cold_table, hot_table):
    ngroup = nz * nyc
    owned, features = cold_table.shape
    slots = hot_ask.shape[-1]
    hot_ask = jnp.pad(hot_ask, ((0, 0), (0, LANES - slots))).reshape(nm, 1, LANES)
    bf16, f32, i32 = jnp.bfloat16, jnp.float32, jnp.int32
    vmem = pl.BlockSpec(memory_space=pltpu.VMEM)
    chunked = pltpu.VMEM((CHUNKS, ngroup, features // CHUNKS), bf16)
    dma = pltpu.SemaphoreType.DMA
    return pl.pallas_call(
        functools.partial(exchange_kernel, nz, nyc, nm),
        out_shape=(
            jax.ShapeDtypeStruct((ngroup, features), bf16),
            jax.ShapeDtypeStruct((1, features), f32),
            jax.ShapeDtypeStruct((nm * slots, features), bf16),
        ),
        in_specs=[vmem] * 4,
        out_specs=(vmem,) * 3,
        scratch_shapes=[
            pltpu.VMEM((nyc, 2, LANES), i32),
            pltpu.VMEM((nz, 1, LANES), i32),
            pltpu.VMEM((nz, 1, LANES), i32),
            pltpu.VMEM((nm, 1, LANES), i32),
            pltpu.VMEM((LANES, LANES), i32),
            pltpu.VMEM((ngroup, owned), bf16),
            pltpu.VMEM((ngroup, owned), bf16),
            chunked,
            chunked,
            chunked,
            chunked,
            pltpu.VMEM((ngroup, features), bf16),
            pltpu.VMEM((ngroup, features), bf16),
            pltpu.VMEM((nz, 1, features), f32),
            pltpu.VMEM((nz, 1, features), f32),
            pltpu.VMEM((nm * slots, features), bf16),
            pltpu.VMEM((nm * slots, features), bf16),
            dma((3,)),
            dma((3,)),
            dma((CHUNKS,)),
            dma((CHUNKS,)),
            dma((CHUNKS,)),
            dma((CHUNKS,)),
            dma((2,)),
            dma((2,)),
            dma,
            dma,
        ],
        compiler_params=pltpu.CompilerParams(
            collective_id=0, has_side_effects=True, vmem_limit_bytes=32 * 1024 * 1024
        ),
    )(ask, hot_ask, cold_table, hot_table)


def per_device(
    nz,
    nyc,
    targets,
    neighbors,
    hot_table,
    hot_req,
    hot_count,
    cold_table,
    cold_owner,
    cold_row,
    w_self,
    w_neigh,
    bias,
):
    members, hot_slots = hot_req.shape[2:]
    groups = nz * nyc
    owners, wanted = cold_owner.reshape(-1), cold_row.reshape(-1)
    requests = owners.shape[0]
    owned = cold_table.shape[0]

    position = jnp.arange(requests, dtype=jnp.int32)
    coded = (position * owned + wanted)[:, None]
    asked = owners[:, None] == jnp.arange(groups, dtype=jnp.int32)[None, :]
    first = jnp.min(jnp.where(asked, coded, requests * owned), axis=0)
    last = jnp.max(jnp.where(asked, coded, -1), axis=0)
    twice = last > first
    first_row = jnp.where(first < requests * owned, first % owned, 0)
    last_row = jnp.where(twice, last % owned, -1)
    ask = jnp.stack([first_row.reshape(nz, nyc).T, last_row.reshape(nz, nyc).T], axis=1)
    ask = jnp.pad(ask, ((0, 0), (0, 0), (0, LANES - nz)))

    cold, extra, hot = exchange(
        nz, nyc, members, ask, hot_req.reshape(members, hot_slots), cold_table, hot_table
    )

    self_part = jnp.dot(targets, w_self, preferred_element_type=jnp.float32)
    columns = jnp.arange(members * hot_slots + requests, dtype=jnp.int32)
    tallies = jnp.sum((neighbors[:, :, None] == columns[None, None, :]).astype(jnp.float32), axis=1)
    keep = (jnp.arange(hot_slots, dtype=jnp.int32)[None, :] < hot_count.reshape(members, 1)).reshape(-1)
    hot_tally = jnp.where(keep[None, :], tallies[:, : members * hot_slots], 0.0).astype(jnp.bfloat16)
    cold_tally = tallies[:, members * hot_slots :].astype(jnp.bfloat16)
    first_at = jnp.where(first < requests * owned, first // owned, -1).reshape(nz, nyc).T.reshape(-1)
    last_at = jnp.max(jnp.where(twice, last // owned, -1))
    place = (position[:, None] == first_at[None, :]).astype(jnp.bfloat16)
    placed = jnp.dot(cold_tally, place, preferred_element_type=jnp.float32).astype(jnp.bfloat16)
    second = jnp.sum(jnp.where(position[None, :] == last_at, tallies[:, members * hot_slots :], 0.0), axis=1)
    summed = jnp.dot(hot_tally, hot, preferred_element_type=jnp.float32)
    summed = summed + jnp.dot(placed, cold, preferred_element_type=jnp.float32)
    summed = summed + second[:, None] * extra
    aggregate = (summed / FANOUT).astype(jnp.bfloat16)
    pre = self_part + jnp.dot(aggregate, w_neigh, preferred_element_type=jnp.float32)
    pre = pre + bias
    active = jnp.maximum(pre, 0.0)
    scale = lax.rsqrt(jnp.mean(active * active, axis=-1, keepdims=True) + 1e-06)
    return (active * scale).astype(jnp.bfloat16)


def solution(mesh, nyc=16):
    nz = mesh.shape["group"] // nyc
    return jax.shard_map(
        functools.partial(per_device, nz, nyc),
        mesh=mesh,
        in_specs=(
            P(("group", "member"), None),
            P(("group", "member"), None),
            P("member", None),
            P("group", "member", None, None),
            P("group", "member", None),
            P("group", None),
            P("group", "member", None),
            P("group", "member", None),
            P(),
            P(),
            P(),
        ),
        out_specs=P(("group", "member"), None),
        check_vma=False,
    )
```

time: 130 us -> 78.9 us (0.61)
  Pallas kernels: 0 us -> 60.8 us
  waiting for transfers between devices: 56.6 us -> 0 us
  starting transfers between devices: 46.7 us -> 0 us
  local copies, waits for them, and re-layouts: 9.67 us -> 2.31 us
  other arithmetic: 10.9 us -> 8.73 us
    pallas_call x0 -> x1, Pallas kernels: none -> 60.8 us  [exchange(): pl.pallas_call(functools.partial(exchange_kernel, nz, nyc, nm), out_shape...]
    all_to_all x4 -> x0, waiting for transfers between devices: 56.6 us -> none  [the longest x2 56.5 us: exchange(): lax.all_to_all(buffer, 'group', split_axis=0, concat_axis=0, tiled=True)]
    all_to_all x4 -> x0, starting transfers between devices: 46.7 us -> none  [the longest x2 38.3 us: exchange(): lax.all_to_all(buffer, 'group', split_axis=0, concat_axis=0, tiled=True)]
    gather x4 -> x0, local copies, waits for them, and re-layouts: 6.14 us -> none  [the longest x1 2.63 us: per_device(): jnp.take(hot_table, lax.all_to_all(asked_hot, 'member', split_axis=0, con...]
    select_n x7 -> x0, other arithmetic: 4.99 us -> none  [the longest x2 2.49 us: per_device(): jnp.take(cold_table, asked_cold.reshape(-1), axis=0)]
    scatter x1 -> x0, local copies, waits for them, and re-layouts: 1.55 us -> none  [per_device(): id_buffer = jnp.zeros((groups * CCAP,), jnp.int32).at[flat_slot].set(wanted)]
    all_to_all x2 -> x0, local copies, waits for them, and re-layouts: 1.33 us -> none  [exchange(): lax.all_to_all(buffer, 'group', split_axis=0, concat_axis=0, tiled=True)]
  transfers between devices with their start and end apart: 4 -> 0, of which waited for: 3 -> 0; matrix products, arithmetic and copies ran while one was open for 16% -> 0% of each run, Pallas kernels for 0% -> 0%
where the time goes in v2:
time: 78.9 us; the launch traced here: 78.4 us
  Pallas kernels  60.8 us (77%)
  other arithmetic  8.73 us (11%)
  matrix products  6.46 us (8%)
  local copies, waits for them, and re-layouts  2.31 us (3%)
    pallas_call x1, Pallas kernels, exchange(): pl.pallas_call(functools.partial(exchange_kernel, nz, nyc, nm), out_shape...  60.8 us
    dot_general x1, matrix products, per_device(): self_part = jnp.dot(targets, w_self, preferred_element_type=jnp.float32)  3 us
    dot_general x1, matrix products, per_device(): jnp.dot(aggregate, w_neigh, preferred_element_type=jnp.float32)  2.99 us
    reduce_sum x1, other arithmetic, per_device(): jnp.sum((neighbors[:, :, None] == columns[None, None, :]).astype(jnp.floa...  2.73 us
    convert_element_type x1, other arithmetic, per_device(): return (active * scale).astype(jnp.bfloat16)  2.14 us

profile of v2, /device:TPU:1, one launch (start us, length us, event | category | flops | bytes accessed | tf_op | source)
XLA Modules:
  0.0 78.4 jit_solution(18432702074094253023)
XLA Ops:
  0.0 0.0 copy-start
  0.0 0.0 copy-start.1
  0.0 0.9 %iota_compare_fusion.4 = pred[4,64]{1,0:T(4,128)(4,1)S(1)} fusion(s32[4]{0:T(128)} %bitcast.27), kind=kLoop, calls=%fused_computation.46 | loop fusion | flops 256 | bytes 272 | tf_op jit(solution)/shard_map/lt | solution.py:355
  0.9 0.1 lt.42
  1.0 0.7 multiply_add_fusion
  1.7 0.8 %select_reduce_fusion.2 = (s32[256]{0:T(256)S(1)}, s32[256]{0:T(256)S(1)}) fusion(s32[256]{0:T(256)S(1)} %multiply_add_fusion, s32[256]{0:T(256)} %bitcast.26), kind=kLoop, calls=%fused_computation.21 | loop fusion | flops 327168 | bytes 4096 | tf_op jit(solution)/shard_map/reduce_min | solution.py:340
  2.5 0.6 fusion.22
  3.1 0.6 iota_compare_fusion.5
  3.8 0.7 pad.9
  4.5 0.1 reduce_min.12
  4.5 0.1 copy.26
  4.6 0.1 reduce_max.21
  4.7 0.1 copy.30
  4.8 0.1 eq.65
  4.9 2.7 %convert_reduce_fusion = f32[256,512]{1,0:T(8,128)S(1)} fusion(s32[256,25]{0,1:T(8,128)} %param.12), kind=kLoop, calls=%fused_computation | loop fusion | flops 9699328 | bytes 549888 | tf_op jit(solution)/shard_map/reduce_sum | solution.py:354
  7.7 0.1 select_reduce_fusion
  7.8 0.2 convolution_convert_fusion
  8.0 0.0 copy-done.1
  8.0 0.0 copy-start.2
  8.0 1.1 %copy-done.2 = bf16[512,768]{1,0:T(8,128)(2,1)S(1)} copy-done((bf16[512,768]{1,0:T(8,128)(2,1)S(1)}, bf16[512,768]{1,0:T(8,128)(2,1)}, u32[]{:S(2)}) %copy-start.2) | copy-done | bytes 786456
  9.1 0.0 copy-start.3
  9.1 60.8 %shard_map.109 = (bf16[256,768]{1,0:T(8,128)(2,1)S(1)}, f32[1,768]{1,0:T(1,128)S(1)}, bf16[256,768]{1,0:T(8,128)(2,1)S(1)}) custom-call(s32[16,2,128]{2,1,0:T(2,128)S(1)} %pad.8.ask_ref, s32[4,1,128]{2,1,0:T(1,128)S(1)} %bitcast.21, bf16[512,768]{1,0:T(8,128)(2,1)S(1)} %copy-done.1, bf16[512,768]{1,0:T(8,128)(2,1)S(1)} %copy-done.2), custom_call_target="tpu_custom_call" | custom-call | tf_op jit(solution)/shard_map/pallas_call | solution.py:272
  69.9 0.3 fusion.10
  70.2 0.0 copy-start.4
  70.2 0.0 copy-done.3
  70.3 3.0 %fusion.25 = f32[256,1024]{1,0:T(8,128)} fusion(bf16[256,768]{1,0:T(8,128)(2,1)S(1)} %copy-done.3, bf16[768,1024]{1,0:T(8,128)(2,1)} %param.19), kind=kOutput, calls=%fused_computation.58 | convolution fusion | flops 402653184 | bytes 3014656 | tf_op jit(solution)/shard_map/dot_general | solution.py:352
  73.3 0.0 copy-done
  73.3 0.0 copy-done.4
  73.3 3.0 %multiply_reduce_fusion = (f32[256]{0:T(256)S(1)}, f32[256,1024]{1,0:T(8,128)}) fusion(f32[1024]{0:T(1024)S(1)} %copy-done.4, f32[256,1024]{1,0:T(8,128)} %fusion.25, bf16[768,1024]{1,0:T(8,128)(2,1)S(1)} %copy-done, f32[256,768]{1,0:T(8,128)S(1)} %fusion.10, bf16[256,256]{1,0:T(8,128)(2,1)S(1)} %convolution_convert_fusion, ...), kind=kOutput, calls=%fused_computation.11 | convolution fusion | flops 505609984 | bytes 4989952 | tf_op jit(solution)/shard_map/dot_general | solution.py:367
  76.3 2.1 %multiply_convert_fusion = bf16[256,1024]{1,0:T(8,128)(2,1)} fusion(f32[256,1024]{1,0:T(8,128)} %get-tuple-element.17, f32[256]{0:T(256)S(1)} %add_rsqrt_fusion), kind=kLoop, calls=%fused_computation.10 | loop fusion | flops 524288 | bytes 1573888 | tf_op jit(solution)/shard_map/convert_element_type | solution.py:371
  (5 shorter events, 0.1 us)
Async XLA Ops:
  0.0 73.3 %copy-start = (bf16[768,1024]{1,0:T(8,128)(2,1)S(1)}, bf16[768,1024]{1,0:T(8,128)(2,1)}, u32[]{:S(2)}) copy-start(bf16[768,1024]{1,0:T(8,128)(2,1)} %param.20) | copy-start | bytes 4718596
  0.0 8.0 %copy-start.1 = (bf16[512,768]{1,0:T(8,128)(2,1)S(1)}, bf16[512,768]{1,0:T(8,128)(2,1)}, u32[]{:S(2)}) copy-start(bf16[512,768]{1,0:T(8,128)(2,1)} %table_ref.1) | copy-start | bytes 2359300
  8.0 1.1 %copy-start.2 = (bf16[512,768]{1,0:T(8,128)(2,1)S(1)}, bf16[512,768]{1,0:T(8,128)(2,1)}, u32[]{:S(2)}) copy-start(bf16[512,768]{1,0:T(8,128)(2,1)} %hot_ref.1) | copy-start | bytes 2359300
  9.1 61.1 %copy-start.3 = (bf16[256,768]{1,0:T(8,128)(2,1)S(1)}, bf16[256,768]{1,0:T(8,128)(2,1)}, u32[]{:S(2)}) copy-start(bf16[256,768]{1,0:T(8,128)(2,1)} %param.11) | copy-start | bytes 1179652
  70.2 3.1 %copy-start.4 = (f32[1024]{0:T(1024)S(1)}, f32[1024]{0:T(1024)}, u32[]{:S(2)}) copy-start(f32[1024]{0:T(1024)} %param.21) | copy-start | bytes 12292

commit v3 on v2

v3 whole, which is shorter than its diff:
```python
import functools

import jax
import jax.numpy as jnp
from jax import lax
from jax.experimental import pallas as pl
from jax.experimental.pallas import tpu as pltpu
from jax.sharding import PartitionSpec as P

FANOUT = 25
LANES = 128
CHUNKS = 3
MESH = pl.DeviceIdType.MESH


def wait_bytes(ref, sem):
    pltpu.make_async_copy(ref, ref, sem).wait()


def one_hot(index, width):
    columns = lax.broadcasted_iota(jnp.int32, (index.shape[0], width), 1)
    return (columns == index).astype(jnp.float32).astype(jnp.bfloat16)


def lane_to_rows(row, rows, first):
    wide = jnp.broadcast_to(row, (rows, LANES))
    lane = lax.broadcasted_iota(jnp.int32, (rows, LANES), 1)
    slot = lax.broadcasted_iota(jnp.int32, (rows, LANES), 0)
    return jnp.sum(jnp.where(lane == slot + first, wide, 0), axis=1, keepdims=True)


def exact_dot(a, b):
    return jnp.dot(a, b, preferred_element_type=jnp.float32)


def layer_kernel(
    nz,
    nyc,
    nm,
    targets_hbm,
    near_hbm,
    hot_hbm,
    hot_req_hbm,
    live_hbm,
    table_hbm,
    owner_hbm,
    wanted_hbm,
    w_self_hbm,
    w_neigh_hbm,
    bias_hbm,
    out_ref,
    targets_ref,
    near_ref,
    hot_ref,
    hot_req_ref,
    live_ref,
    table_ref,
    owner_ref,
    wanted_ref,
    w_self_ref,
    w_neigh_ref,
    bias_ref,
    ask,
    hot_ask,
    ids_a,
    ids_b,
    ids_c,
    hot_ids,
    square,
    hits,
    hits_x,
    z_out,
    z_in,
    y_out,
    y_in,
    x_out,
    x_in,
    row_out,
    row_in,
    h_out,
    h_in,
    tally,
    summed,
    total,
    load_sem,
    send_ids,
    recv_ids,
    send_z,
    recv_z,
    send_y,
    recv_y,
    send_x,
    recv_x,
    send_h,
    recv_h,
):
    group, member = lax.axis_index("group"), lax.axis_index("member")
    z, yc = group // nyc, group % nyc
    ngroup = nz * nyc
    owned, features = table_ref.shape
    width = features // CHUNKS
    slots = h_out.shape[0] // nm
    hot_slots = nm * slots
    rows = targets_ref.shape[0]
    bf16, f32, i32 = jnp.bfloat16, jnp.float32, jnp.int32

    def iota(shape, dim):
        return lax.broadcasted_iota(i32, shape, dim)

    def z_peer(step):
        far = nz // 2 - (step + 1) // 2
        return (z + nz + (1 - 2 * (step % 2)) * far) % nz

    def yc_peer(step):
        return (yc + 1 + step) % nyc

    def m_peer(step):
        return (member + 1 + step) % nm

    def to_z(peer):
        return (peer * nyc + yc, member)

    def to_yc(peer):
        return (z * nyc + peer, member)

    def to_m(peer):
        return (group, peer)

    def each(count, body):
        lax.fori_loop(0, count, lambda i, c: (body(i), c)[1], 0)

    def send(source, target, send_sem, recv_sem, device):
        pltpu.make_async_remote_copy(
            src_ref=source, dst_ref=target, send_sem=send_sem, recv_sem=recv_sem, device_id=device, device_id_type=MESH
        ).start()

    def block(peer, count):
        return pl.ds(pl.multiple_of(peer * count, count), count)

    loads = [
        pltpu.make_async_copy(source, target, load_sem.at[number])
        for number, (source, target) in enumerate(
            [
                (owner_hbm, owner_ref),
                (wanted_hbm, wanted_ref),
                (hot_req_hbm, hot_req_ref),
                (live_hbm, live_ref),
                (bias_hbm, bias_ref),
                (hot_hbm, hot_ref),
                (table_hbm, table_ref),
                (near_hbm, near_ref),
                (targets_hbm, targets_ref),
                (w_self_hbm, w_self_ref),
                (w_neigh_hbm, w_neigh_ref),
            ]
        )
    ]
    for load in loads:
        load.start()

    barrier = pltpu.get_barrier_semaphore()

    def greet(device):
        pl.semaphore_signal(barrier, inc=1, device_id=device, device_id_type=MESH)

    each(nyc - 1, lambda i: greet(to_yc(yc_peer(i))))
    each(nz - 1, lambda i: greet(to_z(z_peer(i))))
    each(nm - 1, lambda i: greet(to_m(m_peer(i))))

    for load in loads[:3]:
        load.wait()
    requests = owner_ref.shape[-1]
    owners = owner_ref[0]
    coded = iota((1, requests), 1) * owned + wanted_ref[0]
    asked = jnp.broadcast_to(owners, (ngroup, requests)) == iota((ngroup, requests), 0)
    coded = jnp.broadcast_to(coded, (ngroup, requests))
    first = jnp.min(jnp.where(asked, coded, requests * owned), axis=1, keepdims=True)
    last = jnp.max(jnp.where(asked, coded, -1), axis=1, keepdims=True)
    twice = last > first
    first_row = jnp.where(first < requests * owned, lax.rem(first, owned), 0)
    last_row = jnp.where(twice, lax.rem(last, owned), -1)
    lane = iota((nyc, LANES), 1)
    packed = jnp.zeros((nyc, LANES), i32)
    for peer in range(nz):
        part = slice(peer * nyc, (peer + 1) * nyc)
        packed = jnp.where(lane == peer, first_row[part], packed)
        packed = jnp.where(lane == nz + peer, last_row[part], packed)
    for peer in range(nyc):
        ask[peer] = packed[peer : peer + 1]
    for peer in range(nm):
        hot_ask[peer] = jnp.zeros((1, LANES), i32)
        hot_ask[peer, :, 0:slots] = hot_req_ref[0, 0, peer : peer + 1, :]

    pl.semaphore_wait(barrier, nz + nyc + nm - 3)

    def send_ids_yc(i):
        peer = yc_peer(i)
        send(ask.at[peer], ids_a.at[yc], send_ids.at[0], recv_ids.at[0], to_yc(peer))

    each(nyc - 1, send_ids_yc)

    def send_ids_m(i):
        peer = m_peer(i)
        send(hot_ask.at[peer], hot_ids.at[member], send_ids.at[2], recv_ids.at[2], to_m(peer))

    each(nm - 1, send_ids_m)
    ids_a[yc] = ask[yc]
    hot_ids[member] = hot_ask[member]
    square[...] = jnp.zeros_like(square)

    wait_bytes(ids_a.at[pl.ds(0, nyc - 1)], recv_ids.at[0])
    for peer in range(nyc):
        square[peer : peer + 1, :] = ids_a[peer]
    square[...] = square[...].T
    for peer in range(nz):
        ids_b[peer, :, 0:nyc] = square[peer : peer + 1, 0:nyc]
        ids_b[peer, :, nyc : 2 * nyc] = square[nz + peer : nz + peer + 1, 0:nyc]

    def send_ids_z(i):
        peer = z_peer(i)
        send(ids_b.at[peer], ids_c.at[z], send_ids.at[1], recv_ids.at[1], to_z(peer))

    each(nz - 1, send_ids_z)
    ids_c[z] = ids_b[z]

    wait_bytes(hot_ids.at[pl.ds(0, nm - 1)], recv_ids.at[2])
    loads[5].wait()
    for peer in range(nm):
        wanted_rows = one_hot(lane_to_rows(hot_ids[peer], slots, 0), hot_ref.shape[0])
        h_out[peer * slots : (peer + 1) * slots, :] = exact_dot(wanted_rows, hot_ref[...]).astype(bf16)

    def send_hot(i):
        peer = m_peer(i)
        send(h_out.at[block(peer, slots)], h_in.at[block(member, slots)], send_h, recv_h, to_m(peer))

    each(nm - 1, send_hot)
    h_in[block(member, slots), :] = h_out[block(member, slots), :]

    rows_to = iota((ngroup, ngroup), 0)
    rows_from = iota((ngroup, ngroup), 1)
    turn = (rows_from == lax.rem(rows_to, nz) * nyc + lax.div(rows_to, nz)).astype(f32).astype(bf16)

    loads[6].wait()
    wait_bytes(ids_c.at[pl.ds(0, nz - 1)], recv_ids.at[1])
    for peer in range(nz):
        hits[peer * nyc : (peer + 1) * nyc, :] = one_hot(lane_to_rows(ids_c[peer], nyc, 0), owned)

    def gather_and_send(chunk):
        z_out[chunk] = exact_dot(hits[...], table_ref[:, chunk * width : (chunk + 1) * width]).astype(bf16)

        def send_rows(i):
            peer = z_peer(i)
            send(
                z_out.at[chunk, block(peer, nyc)],
                z_in.at[chunk, block(z, nyc)],
                send_z.at[chunk],
                recv_z.at[chunk],
                to_z(peer),
            )

        each(nz - 1, send_rows)
        z_in[chunk, block(z, nyc), :] = z_out[chunk, block(z, nyc), :]

    gather_and_send(0)

    for peer in range(nz):
        hits_x[peer * nyc : (peer + 1) * nyc, :] = one_hot(lane_to_rows(ids_c[peer], nyc, nyc), owned)
    ordered = exact_dot(turn, hits_x[...]).astype(bf16)
    x_out[...] = exact_dot(ordered, table_ref[...]).astype(bf16)

    def send_extra(i):
        peer = yc_peer(i)
        send(x_out.at[block(peer, nz)], x_in.at[block(yc, nz)], send_x.at[0], recv_x.at[0], to_yc(peer))

    each(nyc - 1, send_extra)
    x_in[block(yc, nz), :] = x_out[block(yc, nz), :]

    for chunk in range(1, CHUNKS):
        gather_and_send(chunk)

    def turn_and_send(chunk):
        wait_bytes(z_in.at[chunk, pl.ds(0, (nz - 1) * nyc)], recv_z.at[chunk])
        y_out[chunk] = exact_dot(turn, z_in[chunk]).astype(bf16)

        def send_rows(i):
            peer = yc_peer(i)
            send(
                y_out.at[chunk, block(peer, nz)],
                y_in.at[chunk, block(yc, nz)],
                send_y.at[chunk],
                recv_y.at[chunk],
                to_yc(peer),
            )

        each(nyc - 1, send_rows)
        y_in[chunk, block(yc, nz), :] = y_out[chunk, block(yc, nz), :]

    loads[7].wait()
    loads[3].wait()
    near = near_ref[...]
    for first_column in range(0, tally.shape[1], LANES):
        span = min(LANES, tally.shape[1] - first_column)
        columns = iota((rows, span), 1) + first_column
        counted = jnp.zeros((rows, span), f32)
        for j in range(near.shape[1]):
            counted = counted + jnp.where(near[:, j : j + 1] == columns, 1.0, 0.0)
        tally[:, first_column : first_column + span] = counted
    slot = iota((1, hot_slots), 1)
    limit = jnp.zeros((1, hot_slots), i32)
    for peer in range(nm):
        limit = jnp.where(lax.div(slot, slots) == peer, live_ref[0, :, peer : peer + 1], limit)
    hot_tally = jnp.where(lax.rem(slot, slots) < limit, tally[:, 0:hot_slots], 0.0).astype(bf16)
    cold_tally = tally[:, hot_slots:]
    position = iota((ngroup, requests), 1)
    place = (position == lax.div(first, owned)).astype(f32).astype(bf16)
    place = exact_dot(turn, place).astype(bf16)
    placed = lax.dot_general(
        cold_tally.astype(bf16), place, (((1,), (1,)), ((), ())), preferred_element_type=f32
    ).astype(bf16)
    last_at = jnp.max(jnp.where(twice, lax.div(last, owned), -1), axis=0, keepdims=True)
    second = jnp.sum(jnp.where(iota((1, requests), 1) == last_at, cold_tally, 0.0), axis=1, keepdims=True)

    for load in loads[8:10]:
        load.wait()
    loads[4].wait()
    total[...] = exact_dot(targets_ref[...], w_self_ref[...]) + bias_ref[...].reshape(1, -1)

    turn_and_send(0)

    wait_bytes(x_in.at[pl.ds(0, (nyc - 1) * nz)], recv_x.at[0])
    target = iota((nz, ngroup), 0)
    source = iota((nz, ngroup), 1)
    pick = (lax.rem(source, nz) == target).astype(f32).astype(bf16)
    picked = exact_dot(pick, x_in[...])
    for peer in range(nz):
        row_out[peer] = picked[peer : peer + 1, :]

    def send_extra_row(i):
        peer = z_peer(i)
        send(row_out.at[peer], row_in.at[z], send_x.at[1], recv_x.at[1], to_z(peer))

    each(nz - 1, send_extra_row)
    row_in[z] = row_out[z]

    wait_bytes(h_in.at[pl.ds(0, (nm - 1) * slots)], recv_h)
    summed[...] = exact_dot(hot_tally, h_in[...])

    for chunk in range(1, CHUNKS):
        turn_and_send(chunk)

    wait_bytes(row_in.at[pl.ds(0, nz - 1)], recv_x.at[1])
    extra = row_in[0]
    for peer in range(1, nz):
        extra = extra + row_in[peer]
    summed[...] = summed[...] + second * extra
    loads[10].wait()
    for chunk in range(CHUNKS):
        part = slice(chunk * width, (chunk + 1) * width)
        wait_bytes(y_in.at[chunk, pl.ds(0, (nyc - 1) * nz)], recv_y.at[chunk])
        aggregate = summed[:, part] + exact_dot(placed, y_in[chunk])
        aggregate = (aggregate * (1.0 / FANOUT)).astype(bf16)
        total[...] = total[...] + exact_dot(aggregate, w_neigh_ref[part, :])
    active = jnp.maximum(total[...], 0.0)
    scale = lax.rsqrt(jnp.mean(active * active, axis=-1, keepdims=True) + 1e-06)
    out_ref[...] = (active * scale).astype(bf16)

    wait_bytes(ids_a.at[pl.ds(0, nyc - 1)], send_ids.at[0])
    wait_bytes(ids_c.at[pl.ds(0, nz - 1)], send_ids.at[1])
    wait_bytes(hot_ids.at[pl.ds(0, nm - 1)], send_ids.at[2])
    wait_bytes(h_in.at[pl.ds(0, (nm - 1) * slots)], send_h)
    wait_bytes(x_in.at[pl.ds(0, (nyc - 1) * nz)], send_x.at[0])
    wait_bytes(row_in.at[pl.ds(0, nz - 1)], send_x.at[1])
    for chunk in range(CHUNKS):
        wait_bytes(z_in.at[chunk, pl.ds(0, (nz - 1) * nyc)], send_z.at[chunk])
        wait_bytes(y_in.at[chunk, pl.ds(0, (nyc - 1) * nz)], send_y.at[chunk])


def per_device(nz, nyc, *args):
    targets, near, hot_table, hot_req, live, cold_table, owner, wanted, w_self, w_neigh, bias = args
    nm, slots = hot_req.shape[2:]
    ngroup = nz * nyc
    owned, features = cold_table.shape
    rows, hidden = targets.shape[0], w_self.shape[1]
    bf16, f32, i32 = jnp.bfloat16, jnp.float32, jnp.int32
    chunked = pltpu.VMEM((CHUNKS, ngroup, features // CHUNKS), bf16)
    dma = pltpu.SemaphoreType.DMA
    return pl.pallas_call(
        functools.partial(layer_kernel, nz, nyc, nm),
        out_shape=jax.ShapeDtypeStruct((rows, hidden), bf16),
        in_specs=[pl.BlockSpec(memory_space=pl.ANY)] * len(args),
        out_specs=pl.BlockSpec(memory_space=pltpu.VMEM),
        scratch_shapes=[pltpu.VMEM(a.shape, a.dtype) for a in args]
        + [
            pltpu.VMEM((nyc, 1, LANES), i32),
            pltpu.VMEM((nm, 1, LANES), i32),
            pltpu.VMEM((nyc, 1, LANES), i32),
            pltpu.VMEM((nz, 1, LANES), i32),
            pltpu.VMEM((nz, 1, LANES), i32),
            pltpu.VMEM((nm, 1, LANES), i32),
            pltpu.VMEM((LANES, LANES), i32),
            pltpu.VMEM((ngroup, owned), bf16),
            pltpu.VMEM((ngroup, owned), bf16),
            chunked,
            chunked,
            chunked,
            chunked,
            pltpu.VMEM((ngroup, features), bf16),
            pltpu.VMEM((ngroup, features), bf16),
            pltpu.VMEM((nz, 1, features), f32),
            pltpu.VMEM((nz, 1, features), f32),
            pltpu.VMEM((nm * slots, features), bf16),
            pltpu.VMEM((nm * slots, features), bf16),
            pltpu.VMEM((rows, nm * slots + owner.shape[-1]), f32),
            pltpu.VMEM((rows, features), f32),
            pltpu.VMEM((rows, hidden), f32),
            dma((len(args),)),
            dma((3,)),
            dma((3,)),
            dma((CHUNKS,)),
            dma((CHUNKS,)),
            dma((CHUNKS,)),
            dma((CHUNKS,)),
            dma((2,)),
            dma((2,)),
            dma,
            dma,
        ],
        compiler_params=pltpu.CompilerParams(
            collective_id=0, has_side_effects=True, vmem_limit_bytes=48 * 1024 * 1024
        ),
        cost_estimate=pl.CostEstimate(
            flops=4 * rows * features * hidden, bytes_accessed=8 * 1024 * 1024, transcendentals=rows
        ),
    )(*args)


def solution(mesh, nyc=16):
    nz = mesh.shape["group"] // nyc
    return jax.shard_map(
        functools.partial(per_device, nz, nyc),
        mesh=mesh,
        in_specs=(
            P(("group", "member"), None),
            P(("group", "member"), None),
            P("member", None),
            P("group", "member", None, None),
            P("group", "member", None),
            P("group", None),
            P("group", "member", None),
            P("group", "member", None),
            P(),
            P(),
            P(),
        ),
        out_specs=P(("group", "member"), None),
        check_vma=False,
    )
```

time: 78.9 us -> 73.5 us (0.932)
  local copies, waits for them, and re-layouts: 2.31 us -> 11.1 us
  other arithmetic: 8.73 us -> 0 us
  matrix products: 6.46 us -> 0 us
  Pallas kernels: 60.8 us -> 61.9 us
    unnamed x10 -> x22, local copies, waits for them, and re-layouts: 1.15 us -> 11.1 us
    dot_general x4 -> x0, matrix products: 6.46 us -> none  [the longest x1 3 us: per_device(): self_part = jnp.dot(targets, w_self, preferred_element_type=jnp.float32)]
    reduce_sum x2 -> x0, other arithmetic: 2.84 us -> none  [the longest x1 2.73 us: per_device(): jnp.sum((neighbors[:, :, None] == columns[None, None, :]).astype(jnp.floa...]
    convert_element_type x1 -> x0, other arithmetic: 2.14 us -> none  [per_device(): return (active * scale).astype(jnp.bfloat16)]
    pallas_call x1, Pallas kernels: 60.8 us -> 61.9 us  [per_device(): pl.pallas_call(functools.partial(layer_kernel, nz, nyc, nm), out_shape=ja...]
    lt x1 -> x0, other arithmetic: 0.88 us -> none  [per_device(): jnp.arange(hot_slots, dtype=jnp.int32)[None, :]]
    reduce_min x1 -> x0, other arithmetic: 0.82 us -> none  [per_device(): first = jnp.min(jnp.where(asked, coded, requests * owned), axis=0)]
where the time goes in v3:
time: 73.5 us; the launch traced here: 73 us
  Pallas kernels  61.9 us (84%)
  local copies, waits for them, and re-layouts  11.1 us (15%)
    pallas_call x1, Pallas kernels, per_device(): pl.pallas_call(functools.partial(layer_kernel, nz, nyc, nm), out_shape=ja...  61.9 us
    unnamed x22, local copies, waits for them, and re-layouts  11.1 us

profile of v3, /device:TPU:1, one launch (start us, length us, event | category | flops | bytes accessed | tf_op | source)
XLA Modules:
  0.0 73.0 jit_solution(5573205317801345583)
XLA Ops:
  0.0 0.9 %copy.12.near_hbm = s32[256,25]{1,0:T(8,128)S(1)} copy(s32[256,25]{0,1:T(8,128)} %param.12) | data formatting | bytes 51200 | tf_op args[1]
  0.9 0.0 copy-start
  0.9 1.4 %copy-done = bf16[768,1024]{1,0:T(8,128)(2,1)S(1)} copy-done((bf16[768,1024]{1,0:T(8,128)(2,1)S(1)}, bf16[768,1024]{1,0:T(8,128)(2,1)}, u32[]{:S(2)}) %copy-start) | copy-done | bytes 1572888
  2.3 0.0 copy-start.1
  2.3 1.4 %copy-done.1 = bf16[768,1024]{1,0:T(8,128)(2,1)S(1)} copy-done((bf16[768,1024]{1,0:T(8,128)(2,1)S(1)}, bf16[768,1024]{1,0:T(8,128)(2,1)}, u32[]{:S(2)}) %copy-start.1) | copy-done | bytes 1572888
  3.7 0.0 copy-start.2
  3.7 1.1 %copy-done.2 = bf16[512,768]{1,0:T(8,128)(2,1)S(1)} copy-done((bf16[512,768]{1,0:T(8,128)(2,1)S(1)}, bf16[512,768]{1,0:T(8,128)(2,1)}, u32[]{:S(2)}) %copy-start.2) | copy-done | bytes 786456
  4.8 0.0 copy-start.3
  4.8 1.1 %copy-done.3 = bf16[512,768]{1,0:T(8,128)(2,1)S(1)} copy-done((bf16[512,768]{1,0:T(8,128)(2,1)S(1)}, bf16[512,768]{1,0:T(8,128)(2,1)}, u32[]{:S(2)}) %copy-start.3) | copy-done | bytes 786456
  6.0 0.0 copy-start.4
  6.0 1.0 %copy-done.4 = bf16[256,768]{1,0:T(8,128)(2,1)S(1)} copy-done((bf16[256,768]{1,0:T(8,128)(2,1)S(1)}, bf16[256,768]{1,0:T(8,128)(2,1)}, u32[]{:S(2)}) %copy-start.4) | copy-done | bytes 393240
  7.0 0.0 copy-start.5
  7.0 0.7 copy-done.5
  7.6 0.0 copy-start.6
  7.6 0.7 copy-done.6
  8.3 0.0 copy-start.7
  8.3 0.7 copy-done.7
  9.0 0.0 copy-start.8
  9.0 0.7 copy-done.8
  9.7 0.0 copy-start.9
  9.7 0.7 copy-done.9
  10.3 61.9 %shard_map.109 = bf16[256,1024]{1,0:T(8,128)(2,1)S(1)} custom-call(bf16[256,768]{1,0:T(8,128)(2,1)S(1)} %copy-done.4, s32[256,25]{1,0:T(8,128)S(1)} %copy.12.near_hbm, bf16[512,768]{1,0:T(8,128)(2,1)S(1)} %copy-done.2, s32[1,1,4,64]{3,2,1,0:T(4,128)S(1)} %copy-done.6, s32[1,1,4]{2,1,0:T(1,128)S(1)} %copy-done.9, bf16[512,768]{1,0:T(8,128)(2,1)S(1)} %copy-done.3, ...), custom_call_target="tpu_custom_call" | custom-call | flops 805306368 | bytes 8388608 | tf_op jit(solution)/shard_map/pallas_call | solution.py:387
  72.3 0.8 %copy.14 = bf16[256,1024]{1,0:T(8,128)(2,1)} copy(bf16[256,1024]{1,0:T(8,128)(2,1)S(1)} %shard_map.109) | data formatting | bytes 1048576
Async XLA Ops:
  0.9 1.4 %copy-start = (bf16[768,1024]{1,0:T(8,128)(2,1)S(1)}, bf16[768,1024]{1,0:T(8,128)(2,1)}, u32[]{:S(2)}) copy-start(bf16[768,1024]{1,0:T(8,128)(2,1)} %w_self_hbm.1) | copy-start | bytes 4718596
  2.3 1.4 %copy-start.1 = (bf16[768,1024]{1,0:T(8,128)(2,1)S(1)}, bf16[768,1024]{1,0:T(8,128)(2,1)}, u32[]{:S(2)}) copy-start(bf16[768,1024]{1,0:T(8,128)(2,1)} %w_neigh_hbm.1) | copy-start | bytes 4718596
  3.7 1.1 %copy-start.2 = (bf16[512,768]{1,0:T(8,128)(2,1)S(1)}, bf16[512,768]{1,0:T(8,128)(2,1)}, u32[]{:S(2)}) copy-start(bf16[512,768]{1,0:T(8,128)(2,1)} %hot_hbm.1) | copy-start | bytes 2359300
  4.8 1.1 %copy-start.3 = (bf16[512,768]{1,0:T(8,128)(2,1)S(1)}, bf16[512,768]{1,0:T(8,128)(2,1)}, u32[]{:S(2)}) copy-start(bf16[512,768]{1,0:T(8,128)(2,1)} %table_hbm.1) | copy-start | bytes 2359300
  6.0 1.0 %copy-start.4 = (bf16[256,768]{1,0:T(8,128)(2,1)S(1)}, bf16[256,768]{1,0:T(8,128)(2,1)}, u32[]{:S(2)}) copy-start(bf16[256,768]{1,0:T(8,128)(2,1)} %targets_hbm.1) | copy-start | bytes 1179652
  7.0 0.7 copy-start.5
  7.6 0.7 copy-start.6
  8.3 0.7 copy-start.7
  9.0 0.7 copy-start.8
  9.7 0.7 copy-start.9

commit v4 on v3

--- a/solution.py
+++ b/solution.py
@@ -31,6 +31,10 @@
 
 def exact_dot(a, b):
     return jnp.dot(a, b, preferred_element_type=jnp.float32)
+
+
+def count_dot(counts, values):
+    return lax.dot_general(counts, values, (((0,), (0,)), ((), ())), preferred_element_type=jnp.float32)
 
 
 def layer_kernel(
@@ -77,6 +81,7 @@
     x_in,
     row_out,
     row_in,
+    extra,
     h_out,
     h_in,
     tally,
@@ -297,28 +302,26 @@
 
     loads[7].wait()
     loads[3].wait()
-    near = near_ref[...]
-    for first_column in range(0, tally.shape[1], LANES):
-        span = min(LANES, tally.shape[1] - first_column)
-        columns = iota((rows, span), 1) + first_column
-        counted = jnp.zeros((rows, span), f32)
-        for j in range(near.shape[1]):
-            counted = counted + jnp.where(near[:, j : j + 1] == columns, 1.0, 0.0)
-        tally[:, first_column : first_column + span] = counted
-    slot = iota((1, hot_slots), 1)
-    limit = jnp.zeros((1, hot_slots), i32)
+    for first_slot in range(0, tally.shape[0], LANES):
+        span = min(LANES, tally.shape[0] - first_slot)
+        numbers = iota((span, rows), 0) + first_slot
+        counted = jnp.zeros((span, rows), f32)
+        for j in range(near_ref.shape[0]):
+            counted = counted + jnp.where(near_ref[j : j + 1, :] == numbers, 1.0, 0.0)
+        tally[first_slot : first_slot + span, :] = counted
+    slot = iota((hot_slots, 1), 0)
+    limit = jnp.zeros((hot_slots, 1), i32)
     for peer in range(nm):
         limit = jnp.where(lax.div(slot, slots) == peer, live_ref[0, :, peer : peer + 1], limit)
-    hot_tally = jnp.where(lax.rem(slot, slots) < limit, tally[:, 0:hot_slots], 0.0).astype(bf16)
-    cold_tally = tally[:, hot_slots:]
+    hot_tally = jnp.where(lax.rem(slot, slots) < limit, tally[0:hot_slots, :], 0.0).astype(bf16)
+    cold_tally = tally[hot_slots:, :]
     position = iota((ngroup, requests), 1)
     place = (position == lax.div(first, owned)).astype(f32).astype(bf16)
     place = exact_dot(turn, place).astype(bf16)
-    placed = lax.dot_general(
-        cold_tally.astype(bf16), place, (((1,), (1,)), ((), ())), preferred_element_type=f32
-    ).astype(bf16)
+    placed = exact_dot(place, cold_tally.astype(bf16)).astype(bf16)
     last_at = jnp.max(jnp.where(twice, lax.div(last, owned), -1), axis=0, keepdims=True)
-    second = jnp.sum(jnp.where(iota((1, requests), 1) == last_at, cold_tally, 0.0), axis=1, keepdims=True)
+    second = jnp.sum(jnp.where(iota((requests, 1), 0) == last_at, cold_tally, 0.0), axis=0, keepdims=True)
+    second = jnp.broadcast_to(second, (nz, rows)).astype(bf16)
 
     for load in loads[8:10]:
         load.wait()
@@ -343,21 +346,20 @@
     row_in[z] = row_out[z]
 
     wait_bytes(h_in.at[pl.ds(0, (nm - 1) * slots)], recv_h)
-    summed[...] = exact_dot(hot_tally, h_in[...])
+    summed[...] = count_dot(hot_tally, h_in[...])
 
     for chunk in range(1, CHUNKS):
         turn_and_send(chunk)
 
     wait_bytes(row_in.at[pl.ds(0, nz - 1)], recv_x.at[1])
-    extra = row_in[0]
-    for peer in range(1, nz):
-        extra = extra + row_in[peer]
-    summed[...] = summed[...] + second * extra
+    for peer in range(nz):
+        extra[peer : peer + 1, :] = row_in[peer]
+    summed[...] = summed[...] + count_dot(second, extra[...].astype(bf16))
     loads[10].wait()
     for chunk in range(CHUNKS):
         part = slice(chunk * width, (chunk + 1) * width)
         wait_bytes(y_in.at[chunk, pl.ds(0, (nyc - 1) * nz)], recv_y.at[chunk])
-        aggregate = summed[:, part] + exact_dot(placed, y_in[chunk])
+        aggregate = summed[:, part] + count_dot(placed, y_in[chunk])
         aggregate = (aggregate * (1.0 / FANOUT)).astype(bf16)
         total[...] = total[...] + exact_dot(aggregate, w_neigh_ref[part, :])
     active = jnp.maximum(total[...], 0.0)
@@ -377,6 +379,7 @@
 
 def per_device(nz, nyc, *args):
     targets, near, hot_table, hot_req, live, cold_table, owner, wanted, w_self, w_neigh, bias = args
+    args = (targets, near.T) + args[2:]
     nm, slots = hot_req.shape[2:]
     ngroup = nz * nyc
     owned, features = cold_table.shape
@@ -387,7 +390,7 @@
     return pl.pallas_call(
         functools.partial(layer_kernel, nz, nyc, nm),
         out_shape=jax.ShapeDtypeStruct((rows, hidden), bf16),
-        in_specs=[pl.BlockSpec(memory_space=pl.ANY)] * len(args),
+        in_specs=[pl.BlockSpec(memory_space=pltpu.HBM)] * len(args),
         out_specs=pl.BlockSpec(memory_space=pltpu.VMEM),
         scratch_shapes=[pltpu.VMEM(a.shape, a.dtype) for a in args]
         + [
@@ -408,9 +411,10 @@
             pltpu.VMEM((ngroup, features), bf16),
             pltpu.VMEM((nz, 1, features), f32),
             pltpu.VMEM((nz, 1, features), f32),
+            pltpu.VMEM((nz, features), f32),
             pltpu.VMEM((nm * slots, features), bf16),
             pltpu.VMEM((nm * slots, features), bf16),
-            pltpu.VMEM((rows, nm * slots + owner.shape[-1]), f32),
+            pltpu.VMEM((nm * slots + owner.shape[-1], rows), f32),
             pltpu.VMEM((rows, features), f32),
             pltpu.VMEM((rows, hidden), f32),
             dma((len(args),)),
@@ -426,7 +430,7 @@
             dma,
         ],
         compiler_params=pltpu.CompilerParams(
-            collective_id=0, has_side_effects=True, vmem_limit_bytes=48 * 1024 * 1024
+            collective_id=0, has_side_effects=True, vmem_limit_bytes=60 * 1024 * 1024
         ),
         cost_estimate=pl.CostEstimate(
             flops=4 * rows * features * hidden, bytes_accessed=8 * 1024 * 1024, transcendentals=rows

time: 73.5 us -> 64 us (0.87)
  local copies, waits for them, and re-layouts: 11.1 us -> 1.87 us
    unnamed x22 -> x1, local copies, waits for them, and re-layouts: 11.1 us -> 1.87 us
where the time goes in v4:
time: 64 us; the launch traced here: 63.8 us
  Pallas kernels  62 us (97%)
  local copies, waits for them, and re-layouts  1.87 us (3%)
    pallas_call x1, Pallas kernels, per_device(): pl.pallas_call(functools.partial(layer_kernel, nz, nyc, nm), out_shape=ja...  62 us
    unnamed x1, local copies, waits for them, and re-layouts  1.87 us

profile of v4, /device:TPU:1, one launch (start us, length us, event | category | flops | bytes accessed | tf_op | source)
XLA Modules:
  0.0 63.8 jit_solution(15561860392119567826)
XLA Ops:
  0.0 62.0 %shard_map.109 = bf16[256,1024]{1,0:T(8,128)(2,1)} custom-call(bf16[256,768]{1,0:T(8,128)(2,1)} %targets_hbm.1, s32[25,256]{1,0:T(8,128)} %bitcast.1, bf16[512,768]{1,0:T(8,128)(2,1)} %hot_hbm.1, s32[1,1,4,64]{3,2,1,0:T(4,128)} %hot_req_hbm.1, s32[1,1,4]{2,1,0:T(1,128)} %live_hbm.1, bf16[512,768]{1,0:T(8,128)(2,1)} %table_hbm.1, s32[1,1,256]{2,1,0:T(1,128)} %owner_hbm.1, ...), custom_call_target="tpu_custom_call" | custom-call | flops 805306368 | bytes 8388608 | tf_op jit(solution)/shard_map/pallas_call | solution.py:390
  62.0 1.9 %copy.13 = bf16[256,1024]{1,0:T(8,128)(2,1)} copy(bf16[256,1024]{1,0:T(8,128)(2,1)} %shard_map.109) | data formatting | bytes 1048576

commit v5 on v3

--- a/solution.py
+++ b/solution.py
@@ -31,6 +31,10 @@
 
 def exact_dot(a, b):
     return jnp.dot(a, b, preferred_element_type=jnp.float32)
+
+
+def count_dot(counts, values):
+    return lax.dot_general(counts, values, (((0,), (0,)), ((), ())), preferred_element_type=jnp.float32)
 
 
 def layer_kernel(
@@ -67,8 +71,8 @@
     ids_c,
     hot_ids,
     square,
+    near_ids,
     hits,
-    hits_x,
     z_out,
     z_in,
     y_out,
@@ -77,6 +81,7 @@
     x_in,
     row_out,
     row_in,
+    extra,
     h_out,
     h_in,
     tally,
@@ -163,8 +168,8 @@
     def greet(device):
         pl.semaphore_signal(barrier, inc=1, device_id=device, device_id_type=MESH)
 
+    each(nz - 1, lambda i: greet(to_z(z_peer(i))))
     each(nyc - 1, lambda i: greet(to_yc(yc_peer(i))))
-    each(nz - 1, lambda i: greet(to_z(z_peer(i))))
     each(nm - 1, lambda i: greet(to_m(m_peer(i))))
 
     for load in loads[:3]:
@@ -180,48 +185,47 @@
     first_row = jnp.where(first < requests * owned, lax.rem(first, owned), 0)
     last_row = jnp.where(twice, lax.rem(last, owned), -1)
     lane = iota((nyc, LANES), 1)
-    packed = jnp.zeros((nyc, LANES), i32)
+    slot = iota((nyc, LANES), 0)
     for peer in range(nz):
         part = slice(peer * nyc, (peer + 1) * nyc)
-        packed = jnp.where(lane == peer, first_row[part], packed)
-        packed = jnp.where(lane == nz + peer, last_row[part], packed)
-    for peer in range(nyc):
-        ask[peer] = packed[peer : peer + 1]
+        packed = jnp.where(lane == slot, first_row[part], 0) + jnp.where(lane == slot + nyc, last_row[part], 0)
+        ask[peer] = jnp.sum(packed, axis=0, keepdims=True)
     for peer in range(nm):
         hot_ask[peer] = jnp.zeros((1, LANES), i32)
         hot_ask[peer, :, 0:slots] = hot_req_ref[0, 0, peer : peer + 1, :]
 
     pl.semaphore_wait(barrier, nz + nyc + nm - 3)
 
-    def send_ids_yc(i):
-        peer = yc_peer(i)
-        send(ask.at[peer], ids_a.at[yc], send_ids.at[0], recv_ids.at[0], to_yc(peer))
-
-    each(nyc - 1, send_ids_yc)
+    def send_ids_z(i):
+        peer = z_peer(i)
+        send(ask.at[peer], ids_a.at[z], send_ids.at[0], recv_ids.at[0], to_z(peer))
+
+    each(nz - 1, send_ids_z)
 
     def send_ids_m(i):
         peer = m_peer(i)
         send(hot_ask.at[peer], hot_ids.at[member], send_ids.at[2], recv_ids.at[2], to_m(peer))
 
     each(nm - 1, send_ids_m)
-    ids_a[yc] = ask[yc]
+    ids_a[z] = ask[z]
     hot_ids[member] = hot_ask[member]
     square[...] = jnp.zeros_like(square)
 
-    wait_bytes(ids_a.at[pl.ds(0, nyc - 1)], recv_ids.at[0])
-    for peer in range(nyc):
-        square[peer : peer + 1, :] = ids_a[peer]
-    square[...] = square[...].T
-    for peer in range(nz):
-        ids_b[peer, :, 0:nyc] = square[peer : peer + 1, 0:nyc]
-        ids_b[peer, :, nyc : 2 * nyc] = square[nz + peer : nz + peer + 1, 0:nyc]
-
-    def send_ids_z(i):
-        peer = z_peer(i)
-        send(ids_b.at[peer], ids_c.at[z], send_ids.at[1], recv_ids.at[1], to_z(peer))
-
-    each(nz - 1, send_ids_z)
-    ids_c[z] = ids_b[z]
+    loads[7].wait()
+    loads[3].wait()
+    for first_slot in range(0, tally.shape[0], LANES):
+        span = min(LANES, tally.shape[0] - first_slot)
+        numbers = iota((span, rows), 0) + first_slot
+        counted = jnp.zeros((span, rows), f32)
+        for j in range(near_ref.shape[0]):
+            counted = counted + jnp.where(near_ref[j : j + 1, :] == numbers, 1.0, 0.0)
+        tally[first_slot : first_slot + span, :] = counted
+    slot = iota((hot_slots, 1), 0)
+    limit = jnp.zeros((hot_slots, 1), i32)
+    for peer in range(nm):
+        limit = jnp.where(lax.div(slot, slots) == peer, live_ref[0, :, peer : peer + 1], limit)
+    hot_tally = jnp.where(lax.rem(slot, slots) < limit, tally[0:hot_slots, :], 0.0).astype(bf16)
+    cold_tally = tally[hot_slots:, :]
 
     wait_bytes(hot_ids.at[pl.ds(0, nm - 1)], recv_ids.at[2])
     loads[5].wait()
@@ -236,17 +240,35 @@
     each(nm - 1, send_hot)
     h_in[block(member, slots), :] = h_out[block(member, slots), :]
 
+    wait_bytes(ids_a.at[pl.ds(0, nz - 1)], recv_ids.at[0])
+    for peer in range(nz):
+        square[peer : peer + 1, :] = ids_a[peer]
+    square[...] = square[...].T
+    for peer in range(nyc):
+        ids_b[peer, :, 0:nz] = square[peer : peer + 1, 0:nz]
+        ids_b[peer, :, nz : 2 * nz] = square[nyc + peer : nyc + peer + 1, 0:nz]
+
+    def send_ids_yc(i):
+        peer = yc_peer(i)
+        send(ids_b.at[peer], ids_c.at[yc], send_ids.at[1], recv_ids.at[1], to_yc(peer))
+
+    each(nyc - 1, send_ids_yc)
+    ids_c[yc] = ids_b[yc]
+
     rows_to = iota((ngroup, ngroup), 0)
     rows_from = iota((ngroup, ngroup), 1)
     turn = (rows_from == lax.rem(rows_to, nz) * nyc + lax.div(rows_to, nz)).astype(f32).astype(bf16)
+    turn_back = (rows_from == lax.rem(rows_to, nyc) * nz + lax.div(rows_to, nyc)).astype(f32).astype(bf16)
 
     loads[6].wait()
-    wait_bytes(ids_c.at[pl.ds(0, nz - 1)], recv_ids.at[1])
-    for peer in range(nz):
-        hits[peer * nyc : (peer + 1) * nyc, :] = one_hot(lane_to_rows(ids_c[peer], nyc, 0), owned)
-
-    def gather_and_send(chunk):
-        z_out[chunk] = exact_dot(hits[...], table_ref[:, chunk * width : (chunk + 1) * width]).astype(bf16)
+    wait_bytes(ids_c.at[pl.ds(0, nyc - 1)], recv_ids.at[1])
+    for peer in range(nyc):
+        near_ids[peer : peer + 1, :] = ids_c[peer]
+    for peer in range(nz):
+        hits[peer * nyc : (peer + 1) * nyc, :] = one_hot(near_ids[:, peer : peer + 1], owned)
+
+    def rows_along_z(chunk, rows_out):
+        z_out[chunk] = rows_out.astype(bf16)
 
         def send_rows(i):
             peer = z_peer(i)
@@ -261,26 +283,8 @@
         each(nz - 1, send_rows)
         z_in[chunk, block(z, nyc), :] = z_out[chunk, block(z, nyc), :]
 
-    gather_and_send(0)
-
-    for peer in range(nz):
-        hits_x[peer * nyc : (peer + 1) * nyc, :] = one_hot(lane_to_rows(ids_c[peer], nyc, nyc), owned)
-    ordered = exact_dot(turn, hits_x[...]).astype(bf16)
-    x_out[...] = exact_dot(ordered, table_ref[...]).astype(bf16)
-
-    def send_extra(i):
-        peer = yc_peer(i)
-        send(x_out.at[block(peer, nz)], x_in.at[block(yc, nz)], send_x.at[0], recv_x.at[0], to_yc(peer))
-
-    each(nyc - 1, send_extra)
-    x_in[block(yc, nz), :] = x_out[block(yc, nz), :]
-
-    for chunk in range(1, CHUNKS):
-        gather_and_send(chunk)
-
-    def turn_and_send(chunk):
-        wait_bytes(z_in.at[chunk, pl.ds(0, (nz - 1) * nyc)], recv_z.at[chunk])
-        y_out[chunk] = exact_dot(turn, z_in[chunk]).astype(bf16)
+    def rows_along_y(chunk, rows_out):
+        y_out[chunk] = rows_out.astype(bf16)
 
         def send_rows(i):
             peer = yc_peer(i)
@@ -295,37 +299,53 @@
         each(nyc - 1, send_rows)
         y_in[chunk, block(yc, nz), :] = y_out[chunk, block(yc, nz), :]
 
-    loads[7].wait()
-    loads[3].wait()
-    near = near_ref[...]
-    for first_column in range(0, tally.shape[1], LANES):
-        span = min(LANES, tally.shape[1] - first_column)
-        columns = iota((rows, span), 1) + first_column
-        counted = jnp.zeros((rows, span), f32)
-        for j in range(near.shape[1]):
-            counted = counted + jnp.where(near[:, j : j + 1] == columns, 1.0, 0.0)
-        tally[:, first_column : first_column + span] = counted
-    slot = iota((1, hot_slots), 1)
-    limit = jnp.zeros((1, hot_slots), i32)
-    for peer in range(nm):
-        limit = jnp.where(lax.div(slot, slots) == peer, live_ref[0, :, peer : peer + 1], limit)
-    hot_tally = jnp.where(lax.rem(slot, slots) < limit, tally[:, 0:hot_slots], 0.0).astype(bf16)
-    cold_tally = tally[:, hot_slots:]
+    def wait_z(chunk):
+        wait_bytes(z_in.at[chunk, pl.ds(0, (nz - 1) * nyc)], recv_z.at[chunk])
+
+    def wait_y(chunk):
+        wait_bytes(y_in.at[chunk, pl.ds(0, (nyc - 1) * nz)], recv_y.at[chunk])
+
+    def features_of(chunk):
+        return slice(chunk * width, (chunk + 1) * width)
+
+    final = CHUNKS - 1
+    rows_along_z(0, exact_dot(hits[...], table_ref[:, features_of(0)]))
+    turned = exact_dot(turn, hits[...]).astype(bf16)
+    rows_along_y(final, exact_dot(turned, table_ref[:, features_of(final)]))
+
+    for peer in range(nyc):
+        hits[peer * nz : (peer + 1) * nz, :] = one_hot(lane_to_rows(ids_c[peer], nz, nz), owned)
+    x_out[...] = exact_dot(hits[...], table_ref[...]).astype(bf16)
+
+    def send_extra(i):
+        peer = yc_peer(i)
+        send(x_out.at[block(peer, nz)], x_in.at[block(yc, nz)], send_x.at[0], recv_x.at[0], to_yc(peer))
+
+    each(nyc - 1, send_extra)
+    x_in[block(yc, nz), :] = x_out[block(yc, nz), :]
+
+    for peer in range(nz):
+        hits[peer * nyc : (peer + 1) * nyc, :] = one_hot(near_ids[:, peer : peer + 1], owned)
+    for chunk in range(1, final):
+        rows_along_z(chunk, exact_dot(hits[...], table_ref[:, features_of(chunk)]))
+
     position = iota((ngroup, requests), 1)
     place = (position == lax.div(first, owned)).astype(f32).astype(bf16)
-    place = exact_dot(turn, place).astype(bf16)
-    placed = lax.dot_general(
-        cold_tally.astype(bf16), place, (((1,), (1,)), ((), ())), preferred_element_type=f32
-    ).astype(bf16)
+    placed = exact_dot(place, cold_tally.astype(bf16)).astype(bf16)
+    placed_turned = exact_dot(turn, placed).astype(bf16)
     last_at = jnp.max(jnp.where(twice, lax.div(last, owned), -1), axis=0, keepdims=True)
-    second = jnp.sum(jnp.where(iota((1, requests), 1) == last_at, cold_tally, 0.0), axis=1, keepdims=True)
+    second = jnp.sum(jnp.where(iota((requests, 1), 0) == last_at, cold_tally, 0.0), axis=0, keepdims=True)
+    second = jnp.broadcast_to(second, (nz, rows)).astype(bf16)
 
     for load in loads[8:10]:
         load.wait()
     loads[4].wait()
     total[...] = exact_dot(targets_ref[...], w_self_ref[...]) + bias_ref[...].reshape(1, -1)
 
-    turn_and_send(0)
+    wait_z(0)
+    rows_along_y(0, exact_dot(turn, z_in[0]))
+    wait_y(final)
+    rows_along_z(final, exact_dot(turn_back, y_in[final]))
 
     wait_bytes(x_in.at[pl.ds(0, (nyc - 1) * nz)], recv_x.at[0])
     target = iota((nz, ngroup), 0)
@@ -343,29 +363,35 @@
     row_in[z] = row_out[z]
 
     wait_bytes(h_in.at[pl.ds(0, (nm - 1) * slots)], recv_h)
-    summed[...] = exact_dot(hot_tally, h_in[...])
-
-    for chunk in range(1, CHUNKS):
-        turn_and_send(chunk)
-
-    wait_bytes(row_in.at[pl.ds(0, nz - 1)], recv_x.at[1])
-    extra = row_in[0]
-    for peer in range(1, nz):
-        extra = extra + row_in[peer]
-    summed[...] = summed[...] + second * extra
+    summed[...] = count_dot(hot_tally, h_in[...])
+
+    for chunk in range(1, final):
+        wait_z(chunk)
+        rows_along_y(chunk, exact_dot(turn, z_in[chunk]))
+
     loads[10].wait()
-    for chunk in range(CHUNKS):
-        part = slice(chunk * width, (chunk + 1) * width)
-        wait_bytes(y_in.at[chunk, pl.ds(0, (nyc - 1) * nz)], recv_y.at[chunk])
-        aggregate = summed[:, part] + exact_dot(placed, y_in[chunk])
+
+    def add_chunk(chunk, counts, rows_in):
+        part = features_of(chunk)
+        aggregate = summed[:, part] + count_dot(counts, rows_in)
         aggregate = (aggregate * (1.0 / FANOUT)).astype(bf16)
         total[...] = total[...] + exact_dot(aggregate, w_neigh_ref[part, :])
+
+    wait_bytes(row_in.at[pl.ds(0, nz - 1)], recv_x.at[1])
+    for peer in range(nz):
+        extra[peer : peer + 1, :] = row_in[peer]
+    summed[...] = summed[...] + count_dot(second, extra[...].astype(bf16))
+    for chunk in range(final):
+        wait_y(chunk)
+        add_chunk(chunk, placed_turned, y_in[chunk])
+    wait_z(final)
+    add_chunk(final, placed, z_in[final])
     active = jnp.maximum(total[...], 0.0)
     scale = lax.rsqrt(jnp.mean(active * active, axis=-1, keepdims=True) + 1e-06)
     out_ref[...] = (active * scale).astype(bf16)
 
-    wait_bytes(ids_a.at[pl.ds(0, nyc - 1)], send_ids.at[0])
-    wait_bytes(ids_c.at[pl.ds(0, nz - 1)], send_ids.at[1])
+    wait_bytes(ids_a.at[pl.ds(0, nz - 1)], send_ids.at[0])
+    wait_bytes(ids_c.at[pl.ds(0, nyc - 1)], send_ids.at[1])
     wait_bytes(hot_ids.at[pl.ds(0, nm - 1)], send_ids.at[2])
     wait_bytes(h_in.at[pl.ds(0, (nm - 1) * slots)], send_h)
     wait_bytes(x_in.at[pl.ds(0, (nyc - 1) * nz)], send_x.at[0])
@@ -377,6 +403,7 @@
 
 def per_device(nz, nyc, *args):
     targets, near, hot_table, hot_req, live, cold_table, owner, wanted, w_self, w_neigh, bias = args
+    args = (targets, near.T) + args[2:]
     nm, slots = hot_req.shape[2:]
     ngroup = nz * nyc
     owned, features = cold_table.shape
@@ -386,19 +413,19 @@
     dma = pltpu.SemaphoreType.DMA
     return pl.pallas_call(
         functools.partial(layer_kernel, nz, nyc, nm),
-        out_shape=jax.ShapeDtypeStruct((rows, hidden), bf16),
-        in_specs=[pl.BlockSpec(memory_space=pl.ANY)] * len(args),
+        out_shape=pltpu.VMEM((rows, hidden), bf16),
+        in_specs=[pl.BlockSpec(memory_space=pltpu.HBM)] * len(args),
         out_specs=pl.BlockSpec(memory_space=pltpu.VMEM),
         scratch_shapes=[pltpu.VMEM(a.shape, a.dtype) for a in args]
         + [
+            pltpu.VMEM((nz, 1, LANES), i32),
+            pltpu.VMEM((nm, 1, LANES), i32),
+            pltpu.VMEM((nz, 1, LANES), i32),
+            pltpu.VMEM((nyc, 1, LANES), i32),
             pltpu.VMEM((nyc, 1, LANES), i32),
             pltpu.VMEM((nm, 1, LANES), i32),
-            pltpu.VMEM((nyc, 1, LANES), i32),
-            pltpu.VMEM((nz, 1, LANES), i32),
-            pltpu.VMEM((nz, 1, LANES), i32),
-            pltpu.VMEM((nm, 1, LANES), i32),
             pltpu.VMEM((LANES, LANES), i32),
-            pltpu.VMEM((ngroup, owned), bf16),
+            pltpu.VMEM((nyc, LANES), i32),
             pltpu.VMEM((ngroup, owned), bf16),
             chunked,
             chunked,
@@ -408,9 +435,10 @@
             pltpu.VMEM((ngroup, features), bf16),
             pltpu.VMEM((nz, 1, features), f32),
             pltpu.VMEM((nz, 1, features), f32),
+            pltpu.VMEM((nz, features), f32),
             pltpu.VMEM((nm * slots, features), bf16),
             pltpu.VMEM((nm * slots, features), bf16),
-            pltpu.VMEM((rows, nm * slots + owner.shape[-1]), f32),
+            pltpu.VMEM((nm * slots + owner.shape[-1], rows), f32),
             pltpu.VMEM((rows, features), f32),
             pltpu.VMEM((rows, hidden), f32),
             dma((len(args),)),
@@ -426,7 +454,7 @@
             dma,
         ],
         compiler_params=pltpu.CompilerParams(
-            collective_id=0, has_side_effects=True, vmem_limit_bytes=48 * 1024 * 1024
+            collective_id=0, has_side_effects=True, vmem_limit_bytes=60 * 1024 * 1024
         ),
         cost_estimate=pl.CostEstimate(
             flops=4 * rows * features * hidden, bytes_accessed=8 * 1024 * 1024, transcendentals=rows

time: 73.5 us -> 60.8 us (0.83)
  local copies, waits for them, and re-layouts: 11.1 us -> 0.8 us
  Pallas kernels: 61.9 us -> 59.9 us
    unnamed x22 -> x1, local copies, waits for them, and re-layouts: 11.1 us -> 0.8 us
    pallas_call x1, Pallas kernels: 61.9 us -> 59.9 us  [per_device(): pl.pallas_call(functools.partial(layer_kernel, nz, nyc, nm), out_shape=pl...]
where the time goes in v5:
time: 60.8 us; the launch traced here: 60.7 us
  Pallas kernels  59.9 us (99%)
  local copies, waits for them, and re-layouts  0.8 us (1%)
    pallas_call x1, Pallas kernels, per_device(): pl.pallas_call(functools.partial(layer_kernel, nz, nyc, nm), out_shape=pl...  59.9 us

profile of v5, /device:TPU:1, one launch (start us, length us, event | category | flops | bytes accessed | tf_op | source)
XLA Modules:
  0.0 60.7 jit_solution(13089237129356163804)
XLA Ops:
  0.0 59.9 %shard_map.109 = bf16[256,1024]{1,0:T(8,128)(2,1)S(1)} custom-call(bf16[256,768]{1,0:T(8,128)(2,1)} %targets_hbm.1, s32[25,256]{1,0:T(8,128)} %bitcast.1, bf16[512,768]{1,0:T(8,128)(2,1)} %hot_hbm.1, s32[1,1,4,64]{3,2,1,0:T(4,128)} %hot_req_hbm.1, s32[1,1,4]{2,1,0:T(1,128)} %live_hbm.1, bf16[512,768]{1,0:T(8,128)(2,1)} %table_hbm.1, s32[1,1,256]{2,1,0:T(1,128)} %owner_hbm.1, ...), custom_call_target="tpu_custom_call" | custom-call | flops 805306368 | bytes 8388608 | tf_op jit(solution)/shard_map/pallas_call | solution.py:414
  59.9 0.8 %copy.13 = bf16[256,1024]{1,0:T(8,128)(2,1)} copy(bf16[256,1024]{1,0:T(8,128)(2,1)S(1)} %shard_map.109) | data formatting | bytes 1048576

commit v6 on v5

--- a/solution.py
+++ b/solution.py
@@ -9,7 +9,9 @@
 
 FANOUT = 25
 LANES = 128
-CHUNKS = 3
+PIECES = 6
+Z_FIRST = ((0, 2), (2, 1))
+Y_FIRST = ((3, 1), (4, 2))
 MESH = pl.DeviceIdType.MESH
 
 
@@ -71,13 +73,15 @@
     ids_c,
     hot_ids,
     square,
-    near_ids,
     hits,
+    hits_x,
     z_out,
     z_in,
     y_out,
     y_in,
     x_out,
+    x_core,
+    x_send,
     x_in,
     row_out,
     row_in,
@@ -90,6 +94,7 @@
     load_sem,
     send_ids,
     recv_ids,
+    recv_ids_z,
     send_z,
     recv_z,
     send_y,
@@ -101,9 +106,11 @@
 ):
     group, member = lax.axis_index("group"), lax.axis_index("member")
     z, yc = group // nyc, group % nyc
+    y, core, ny = yc // 2, yc % 2, nyc // 2
     ngroup = nz * nyc
+    half = ny * nz
     owned, features = table_ref.shape
-    width = features // CHUNKS
+    width = features // PIECES
     slots = h_out.shape[0] // nm
     hot_slots = nm * slots
     rows = targets_ref.shape[0]
@@ -185,29 +192,31 @@
     first_row = jnp.where(first < requests * owned, lax.rem(first, owned), 0)
     last_row = jnp.where(twice, lax.rem(last, owned), -1)
     lane = iota((nyc, LANES), 1)
-    slot = iota((nyc, LANES), 0)
+    packed = jnp.zeros((nyc, LANES), i32)
     for peer in range(nz):
         part = slice(peer * nyc, (peer + 1) * nyc)
-        packed = jnp.where(lane == slot, first_row[part], 0) + jnp.where(lane == slot + nyc, last_row[part], 0)
-        ask[peer] = jnp.sum(packed, axis=0, keepdims=True)
+        packed = jnp.where(lane == peer, first_row[part], packed)
+        packed = jnp.where(lane == nz + peer, last_row[part], packed)
+    for peer in range(nyc):
+        ask[peer] = packed[peer : peer + 1]
     for peer in range(nm):
         hot_ask[peer] = jnp.zeros((1, LANES), i32)
         hot_ask[peer, :, 0:slots] = hot_req_ref[0, 0, peer : peer + 1, :]
 
     pl.semaphore_wait(barrier, nz + nyc + nm - 3)
 
-    def send_ids_z(i):
-        peer = z_peer(i)
-        send(ask.at[peer], ids_a.at[z], send_ids.at[0], recv_ids.at[0], to_z(peer))
-
-    each(nz - 1, send_ids_z)
+    def send_ids_yc(i):
+        peer = yc_peer(i)
+        send(ask.at[peer], ids_a.at[yc], send_ids.at[0], recv_ids.at[0], to_yc(peer))
+
+    each(nyc - 1, send_ids_yc)
 
     def send_ids_m(i):
         peer = m_peer(i)
         send(hot_ask.at[peer], hot_ids.at[member], send_ids.at[2], recv_ids.at[2], to_m(peer))
 
     each(nm - 1, send_ids_m)
-    ids_a[z] = ask[z]
+    ids_a[yc] = ask[yc]
     hot_ids[member] = hot_ask[member]
     square[...] = jnp.zeros_like(square)
 
@@ -240,20 +249,20 @@
     each(nm - 1, send_hot)
     h_in[block(member, slots), :] = h_out[block(member, slots), :]
 
-    wait_bytes(ids_a.at[pl.ds(0, nz - 1)], recv_ids.at[0])
-    for peer in range(nz):
+    wait_bytes(ids_a.at[pl.ds(0, nyc - 1)], recv_ids.at[0])
+    for peer in range(nyc):
         square[peer : peer + 1, :] = ids_a[peer]
     square[...] = square[...].T
-    for peer in range(nyc):
-        ids_b[peer, :, 0:nz] = square[peer : peer + 1, 0:nz]
-        ids_b[peer, :, nz : 2 * nz] = square[nyc + peer : nyc + peer + 1, 0:nz]
-
-    def send_ids_yc(i):
-        peer = yc_peer(i)
-        send(ids_b.at[peer], ids_c.at[yc], send_ids.at[1], recv_ids.at[1], to_yc(peer))
-
-    each(nyc - 1, send_ids_yc)
-    ids_c[yc] = ids_b[yc]
+    for peer in range(nz):
+        ids_b[peer, :, 0:nyc] = square[peer : peer + 1, 0:nyc]
+        ids_b[peer, :, nyc : 2 * nyc] = square[nz + peer : nz + peer + 1, 0:nyc]
+
+    def send_ids_z(i):
+        peer = z_peer(i)
+        send(ids_b.at[peer], ids_c.at[z], send_ids.at[1], recv_ids_z.at[z], to_z(peer))
+
+    each(nz - 1, send_ids_z)
+    ids_c[z] = ids_b[z]
 
     rows_to = iota((ngroup, ngroup), 0)
     rows_from = iota((ngroup, ngroup), 1)
@@ -261,73 +270,112 @@
     turn_back = (rows_from == lax.rem(rows_to, nyc) * nz + lax.div(rows_to, nyc)).astype(f32).astype(bf16)
 
     loads[6].wait()
-    wait_bytes(ids_c.at[pl.ds(0, nyc - 1)], recv_ids.at[1])
-    for peer in range(nyc):
-        near_ids[peer : peer + 1, :] = ids_c[peer]
-    for peer in range(nz):
-        hits[peer * nyc : (peer + 1) * nyc, :] = one_hot(near_ids[:, peer : peer + 1], owned)
+    def features_of(chunk):
+        return slice(chunk[0] * width, (chunk[0] + chunk[1]) * width)
+
+    def pieces_of(chunk):
+        return pl.ds(chunk[0], chunk[1])
+
+    def keep(ref, chunk, rows_of, values):
+        for piece in range(chunk[1]):
+            ref[chunk[0] + piece, rows_of, :] = values[:, piece * width : (piece + 1) * width].astype(bf16)
+
+    def whole(ref, chunk):
+        return jnp.concatenate([ref[chunk[0] + piece] for piece in range(chunk[1])], axis=1)
+
+    offsets = [0]
+    for far in range(1, nz // 2):
+        offsets += [far, -far]
+    offsets += [nz // 2]
+    peers = [lax.rem(z + (nz + offset), nz) for offset in offsets]
+
+    def send_batch(chunk, begin, end):
+        for number in range(begin, end):
+            held = pl.ds(number * nyc, nyc)
+            if offsets[number]:
+                send(
+                    z_out.at[pieces_of(chunk), held],
+                    z_in.at[pieces_of(chunk), block(z, nyc)],
+                    send_z.at[chunk[0]],
+                    recv_z.at[chunk[0]],
+                    to_z(peers[number]),
+                )
+            else:
+                z_in[pieces_of(chunk), block(z, nyc), :] = z_out[pieces_of(chunk), held, :]
+
+    early = sum(count for _, count in Z_FIRST)
+    cuts = [cut for cut in (0, 5, 9, 13) if cut < nz] + [nz]
+    batches = list(zip(cuts[:-1], cuts[1:]))
+    for begin, end in batches:
+        wanted_rows = []
+        for number in range(begin, end):
+            peer = peers[number]
+            if offsets[number]:
+                wait_bytes(ids_c.at[peer], recv_ids_z.at[peer])
+            row = ids_c[peer]
+            wanted_rows.append(one_hot(lane_to_rows(row, nyc, 0), owned))
+            hits[block(peer, nyc), :] = wanted_rows[-1]
+            hits_x[block(peer, nyc), :] = one_hot(lane_to_rows(row, nyc, nyc), owned)
+        found = exact_dot(jnp.concatenate(wanted_rows, axis=0), table_ref[:, 0 : early * width])
+        keep(z_out, (0, early), slice(begin * nyc, end * nyc), found)
+        send_batch(Z_FIRST[0], begin, end)
+        if begin == 0:
+            for chunk in Z_FIRST[1:]:
+                send_batch(chunk, begin, end)
 
     def rows_along_z(chunk, rows_out):
-        z_out[chunk] = rows_out.astype(bf16)
+        keep(z_out, chunk, slice(0, ngroup), rows_out)
 
         def send_rows(i):
             peer = z_peer(i)
             send(
-                z_out.at[chunk, block(peer, nyc)],
-                z_in.at[chunk, block(z, nyc)],
-                send_z.at[chunk],
-                recv_z.at[chunk],
+                z_out.at[pieces_of(chunk), block(peer, nyc)],
+                z_in.at[pieces_of(chunk), block(z, nyc)],
+                send_z.at[chunk[0]],
+                recv_z.at[chunk[0]],
                 to_z(peer),
             )
 
         each(nz - 1, send_rows)
-        z_in[chunk, block(z, nyc), :] = z_out[chunk, block(z, nyc), :]
+        z_in[pieces_of(chunk), block(z, nyc), :] = z_out[pieces_of(chunk), block(z, nyc), :]
 
     def rows_along_y(chunk, rows_out):
-        y_out[chunk] = rows_out.astype(bf16)
+        keep(y_out, chunk, slice(0, ngroup), rows_out)
 
         def send_rows(i):
             peer = yc_peer(i)
             send(
-                y_out.at[chunk, block(peer, nz)],
-                y_in.at[chunk, block(yc, nz)],
-                send_y.at[chunk],
-                recv_y.at[chunk],
+                y_out.at[pieces_of(chunk), block(peer, nz)],
+                y_in.at[pieces_of(chunk), block(yc, nz)],
+                send_y.at[chunk[0]],
+                recv_y.at[chunk[0]],
                 to_yc(peer),
             )
 
         each(nyc - 1, send_rows)
-        y_in[chunk, block(yc, nz), :] = y_out[chunk, block(yc, nz), :]
-
-    def wait_z(chunk):
-        wait_bytes(z_in.at[chunk, pl.ds(0, (nz - 1) * nyc)], recv_z.at[chunk])
-
-    def wait_y(chunk):
-        wait_bytes(y_in.at[chunk, pl.ds(0, (nyc - 1) * nz)], recv_y.at[chunk])
-
-    def features_of(chunk):
-        return slice(chunk * width, (chunk + 1) * width)
-
-    final = CHUNKS - 1
-    rows_along_z(0, exact_dot(hits[...], table_ref[:, features_of(0)]))
+        y_in[pieces_of(chunk), block(yc, nz), :] = y_out[pieces_of(chunk), block(yc, nz), :]
+
+    def wait_z(chunk, sem=None):
+        sem = recv_z if sem is None else sem
+        wait_bytes(z_in.at[pieces_of(chunk), pl.ds(0, (nz - 1) * nyc)], sem.at[chunk[0]])
+
+    def wait_y(chunk, sem=None):
+        sem = recv_y if sem is None else sem
+        wait_bytes(y_in.at[pieces_of(chunk), pl.ds(0, (nyc - 1) * nz)], sem.at[chunk[0]])
+
     turned = exact_dot(turn, hits[...]).astype(bf16)
-    rows_along_y(final, exact_dot(turned, table_ref[:, features_of(final)]))
-
-    for peer in range(nyc):
-        hits[peer * nz : (peer + 1) * nz, :] = one_hot(lane_to_rows(ids_c[peer], nz, nz), owned)
-    x_out[...] = exact_dot(hits[...], table_ref[...]).astype(bf16)
-
-    def send_extra(i):
-        peer = yc_peer(i)
-        send(x_out.at[block(peer, nz)], x_in.at[block(yc, nz)], send_x.at[0], recv_x.at[0], to_yc(peer))
-
-    each(nyc - 1, send_extra)
-    x_in[block(yc, nz), :] = x_out[block(yc, nz), :]
-
-    for peer in range(nz):
-        hits[peer * nyc : (peer + 1) * nyc, :] = one_hot(near_ids[:, peer : peer + 1], owned)
-    for chunk in range(1, final):
-        rows_along_z(chunk, exact_dot(hits[...], table_ref[:, features_of(chunk)]))
+    rows_along_y(Y_FIRST[0], exact_dot(turned, table_ref[:, features_of(Y_FIRST[0])]))
+    for begin, end in batches[:0:-1]:
+        for chunk in Z_FIRST[1:]:
+            send_batch(chunk, begin, end)
+    for chunk in Y_FIRST[1:]:
+        rows_along_y(chunk, exact_dot(turned, table_ref[:, features_of(chunk)]))
+
+    spread = (rows_from == lax.rem(rows_to, nz) * nyc + lax.rem(lax.div(rows_to, nz), ny) * 2 + lax.div(rows_to, half))
+    spread = spread.astype(f32).astype(bf16)
+    turned = exact_dot(spread, hits_x[...]).astype(bf16)
+    x_out[...] = exact_dot(turned, table_ref[...]).astype(bf16)
+    send(x_out.at[block(1 - core, half)], x_core, send_x.at[0], recv_x.at[0], to_yc(y * 2 + 1 - core))
 
     position = iota((ngroup, requests), 1)
     place = (position == lax.div(first, owned)).astype(f32).astype(bf16)
@@ -337,19 +385,35 @@
     second = jnp.sum(jnp.where(iota((requests, 1), 0) == last_at, cold_tally, 0.0), axis=0, keepdims=True)
     second = jnp.broadcast_to(second, (nz, rows)).astype(bf16)
 
+    wait_bytes(x_core, recv_x.at[0])
+    x_send[...] = x_out[block(core, half), :] + x_core[...]
+
+    def send_extra(i):
+        peer = lax.rem(y + 1 + i, ny)
+        send(x_send.at[block(peer, nz)], x_in.at[block(y, nz)], send_x.at[1], recv_x.at[1], to_yc(peer * 2 + core))
+
+    each(ny - 1, send_extra)
+    x_in[block(y, nz), :] = x_send[block(y, nz), :]
+
     for load in loads[8:10]:
         load.wait()
     loads[4].wait()
     total[...] = exact_dot(targets_ref[...], w_self_ref[...]) + bias_ref[...].reshape(1, -1)
 
-    wait_z(0)
-    rows_along_y(0, exact_dot(turn, z_in[0]))
-    wait_y(final)
-    rows_along_z(final, exact_dot(turn_back, y_in[final]))
-
-    wait_bytes(x_in.at[pl.ds(0, (nyc - 1) * nz)], recv_x.at[0])
-    target = iota((nz, ngroup), 0)
-    source = iota((nz, ngroup), 1)
+    wait_y(Y_FIRST[0])
+    rows_along_z(Y_FIRST[0], exact_dot(turn_back, whole(y_in, Y_FIRST[0])))
+    wait_z(Z_FIRST[0])
+    rows_along_y(Z_FIRST[0], exact_dot(turn, whole(z_in, Z_FIRST[0])))
+    for chunk in Y_FIRST[1:]:
+        wait_y(chunk)
+        rows_along_z(chunk, exact_dot(turn_back, whole(y_in, chunk)))
+    for chunk in Z_FIRST[1:]:
+        wait_z(chunk)
+        rows_along_y(chunk, exact_dot(turn, whole(z_in, chunk)))
+
+    wait_bytes(x_in.at[pl.ds(0, (ny - 1) * nz)], recv_x.at[1])
+    target = iota((nz, half), 0)
+    source = iota((nz, half), 1)
     pick = (lax.rem(source, nz) == target).astype(f32).astype(bf16)
     picked = exact_dot(pick, x_in[...])
     for peer in range(nz):
@@ -357,17 +421,13 @@
 
     def send_extra_row(i):
         peer = z_peer(i)
-        send(row_out.at[peer], row_in.at[z], send_x.at[1], recv_x.at[1], to_z(peer))
+        send(row_out.at[peer], row_in.at[z], send_x.at[2], recv_x.at[2], to_z(peer))
 
     each(nz - 1, send_extra_row)
     row_in[z] = row_out[z]
 
     wait_bytes(h_in.at[pl.ds(0, (nm - 1) * slots)], recv_h)
     summed[...] = count_dot(hot_tally, h_in[...])
-
-    for chunk in range(1, final):
-        wait_z(chunk)
-        rows_along_y(chunk, exact_dot(turn, z_in[chunk]))
 
     loads[10].wait()
 
@@ -377,28 +437,34 @@
         aggregate = (aggregate * (1.0 / FANOUT)).astype(bf16)
         total[...] = total[...] + exact_dot(aggregate, w_neigh_ref[part, :])
 
-    wait_bytes(row_in.at[pl.ds(0, nz - 1)], recv_x.at[1])
+    wait_bytes(row_in.at[pl.ds(0, nz - 1)], recv_x.at[2])
     for peer in range(nz):
         extra[peer : peer + 1, :] = row_in[peer]
     summed[...] = summed[...] + count_dot(second, extra[...].astype(bf16))
-    for chunk in range(final):
+    wait_y(Z_FIRST[0])
+    add_chunk(Z_FIRST[0], placed_turned, whole(y_in, Z_FIRST[0]))
+    wait_z(Y_FIRST[0])
+    add_chunk(Y_FIRST[0], placed, whole(z_in, Y_FIRST[0]))
+    for chunk in Z_FIRST[1:]:
         wait_y(chunk)
-        add_chunk(chunk, placed_turned, y_in[chunk])
-    wait_z(final)
-    add_chunk(final, placed, z_in[final])
+        add_chunk(chunk, placed_turned, whole(y_in, chunk))
+    for chunk in Y_FIRST[1:]:
+        wait_z(chunk)
+        add_chunk(chunk, placed, whole(z_in, chunk))
     active = jnp.maximum(total[...], 0.0)
     scale = lax.rsqrt(jnp.mean(active * active, axis=-1, keepdims=True) + 1e-06)
     out_ref[...] = (active * scale).astype(bf16)
 
-    wait_bytes(ids_a.at[pl.ds(0, nz - 1)], send_ids.at[0])
-    wait_bytes(ids_c.at[pl.ds(0, nyc - 1)], send_ids.at[1])
+    wait_bytes(ids_a.at[pl.ds(0, nyc - 1)], send_ids.at[0])
+    wait_bytes(ids_c.at[pl.ds(0, nz - 1)], send_ids.at[1])
     wait_bytes(hot_ids.at[pl.ds(0, nm - 1)], send_ids.at[2])
     wait_bytes(h_in.at[pl.ds(0, (nm - 1) * slots)], send_h)
-    wait_bytes(x_in.at[pl.ds(0, (nyc - 1) * nz)], send_x.at[0])
-    wait_bytes(row_in.at[pl.ds(0, nz - 1)], send_x.at[1])
-    for chunk in range(CHUNKS):
-        wait_bytes(z_in.at[chunk, pl.ds(0, (nz - 1) * nyc)], send_z.at[chunk])
-        wait_bytes(y_in.at[chunk, pl.ds(0, (nyc - 1) * nz)], send_y.at[chunk])
+    wait_bytes(x_core, send_x.at[0])
+    wait_bytes(x_in.at[pl.ds(0, (ny - 1) * nz)], send_x.at[1])
+    wait_bytes(row_in.at[pl.ds(0, nz - 1)], send_x.at[2])
+    for chunk in Z_FIRST + Y_FIRST:
+        wait_z(chunk, send_z)
+        wait_y(chunk, send_y)
 
 
 def per_device(nz, nyc, *args):
@@ -409,7 +475,7 @@
     owned, features = cold_table.shape
     rows, hidden = targets.shape[0], w_self.shape[1]
     bf16, f32, i32 = jnp.bfloat16, jnp.float32, jnp.int32
-    chunked = pltpu.VMEM((CHUNKS, ngroup, features // CHUNKS), bf16)
+    chunked = pltpu.VMEM((PIECES, ngroup, features // PIECES), bf16)
     dma = pltpu.SemaphoreType.DMA
     return pl.pallas_call(
         functools.partial(layer_kernel, nz, nyc, nm),
@@ -418,21 +484,23 @@
         out_specs=pl.BlockSpec(memory_space=pltpu.VMEM),
         scratch_shapes=[pltpu.VMEM(a.shape, a.dtype) for a in args]
         + [
+            pltpu.VMEM((nyc, 1, LANES), i32),
+            pltpu.VMEM((nm, 1, LANES), i32),
+            pltpu.VMEM((nyc, 1, LANES), i32),
+            pltpu.VMEM((nz, 1, LANES), i32),
             pltpu.VMEM((nz, 1, LANES), i32),
             pltpu.VMEM((nm, 1, LANES), i32),
-            pltpu.VMEM((nz, 1, LANES), i32),
-            pltpu.VMEM((nyc, 1, LANES), i32),
-            pltpu.VMEM((nyc, 1, LANES), i32),
-            pltpu.VMEM((nm, 1, LANES), i32),
             pltpu.VMEM((LANES, LANES), i32),
-            pltpu.VMEM((nyc, LANES), i32),
+            pltpu.VMEM((ngroup, owned), bf16),
             pltpu.VMEM((ngroup, owned), bf16),
             chunked,
             chunked,
             chunked,
             chunked,
             pltpu.VMEM((ngroup, features), bf16),
-            pltpu.VMEM((ngroup, features), bf16),
+            pltpu.VMEM((ngroup // 2, features), bf16),
+            pltpu.VMEM((ngroup // 2, features), bf16),
+            pltpu.VMEM((ngroup // 2, features), bf16),
             pltpu.VMEM((nz, 1, features), f32),
             pltpu.VMEM((nz, 1, features), f32),
             pltpu.VMEM((nz, features), f32),
@@ -444,12 +512,13 @@
             dma((len(args),)),
             dma((3,)),
             dma((3,)),
-            dma((CHUNKS,)),
-            dma((CHUNKS,)),
-            dma((CHUNKS,)),
-            dma((CHUNKS,)),
-            dma((2,)),
-            dma((2,)),
+            dma((nz,)),
+            dma((PIECES,)),
+            dma((PIECES,)),
+            dma((PIECES,)),
+            dma((PIECES,)),
+            dma((3,)),
+            dma((3,)),
             dma,
             dma,
         ],

time: 60.8 us -> 59.2 us (0.974)
  Pallas kernels: 59.9 us -> 58.1 us
    pallas_call x1, Pallas kernels: 59.9 us -> 58.1 us  [per_device(): pl.pallas_call(functools.partial(layer_kernel, nz, nyc, nm), out_shape=pl...]
where the time goes in v6:
time: 59.2 us; the launch traced here: 58.9 us
  Pallas kernels  58.1 us (98%)
  local copies, waits for them, and re-layouts  0.8 us (1%)
    pallas_call x1, Pallas kernels, per_device(): pl.pallas_call(functools.partial(layer_kernel, nz, nyc, nm), out_shape=pl...  58.1 us

profile of v6, /device:TPU:1, one launch (start us, length us, event | category | flops | bytes accessed | tf_op | source)
XLA Modules:
  0.0 58.9 jit_solution(17725746061864233779)
XLA Ops:
  0.0 58.1 %shard_map.109 = bf16[256,1024]{1,0:T(8,128)(2,1)S(1)} custom-call(bf16[256,768]{1,0:T(8,128)(2,1)} %targets_hbm.1, s32[25,256]{1,0:T(8,128)} %bitcast.1, bf16[512,768]{1,0:T(8,128)(2,1)} %hot_hbm.1, s32[1,1,4,64]{3,2,1,0:T(4,128)} %hot_req_hbm.1, s32[1,1,4]{2,1,0:T(1,128)} %live_hbm.1, bf16[512,768]{1,0:T(8,128)(2,1)} %table_hbm.1, s32[1,1,256]{2,1,0:T(1,128)} %owner_hbm.1, ...), custom_call_target="tpu_custom_call" | custom-call | flops 805306368 | bytes 8388608 | tf_op jit(solution)/shard_map/pallas_call | solution.py:480
  58.1 0.8 %copy.13 = bf16[256,1024]{1,0:T(8,128)(2,1)} copy(bf16[256,1024]{1,0:T(8,128)(2,1)S(1)} %shard_map.109) | data formatting | bytes 1048576

commit v7 on v6

--- a/solution.py
+++ b/solution.py
@@ -11,7 +11,7 @@
 LANES = 128
 PIECES = 6
 Z_FIRST = ((0, 2), (2, 1))
-Y_FIRST = ((3, 1), (4, 2))
+Y_FIRST = ((3, 1), (4, 1), (5, 1))
 MESH = pl.DeviceIdType.MESH
 
 
@@ -123,8 +123,12 @@
         far = nz // 2 - (step + 1) // 2
         return (z + nz + (1 - 2 * (step % 2)) * far) % nz
 
+    def y_peer(step):
+        far = ny // 2 - (step + 1) // 2
+        return (y + ny + (1 - 2 * (step % 2)) * far) % ny
+
     def yc_peer(step):
-        return (yc + 1 + step) % nyc
+        return y_peer(step // 2) * 2 + (core + 1 + step) % 2
 
     def m_peer(step):
         return (member + 1 + step) % nm
@@ -236,19 +240,6 @@
     hot_tally = jnp.where(lax.rem(slot, slots) < limit, tally[0:hot_slots, :], 0.0).astype(bf16)
     cold_tally = tally[hot_slots:, :]
 
-    wait_bytes(hot_ids.at[pl.ds(0, nm - 1)], recv_ids.at[2])
-    loads[5].wait()
-    for peer in range(nm):
-        wanted_rows = one_hot(lane_to_rows(hot_ids[peer], slots, 0), hot_ref.shape[0])
-        h_out[peer * slots : (peer + 1) * slots, :] = exact_dot(wanted_rows, hot_ref[...]).astype(bf16)
-
-    def send_hot(i):
-        peer = m_peer(i)
-        send(h_out.at[block(peer, slots)], h_in.at[block(member, slots)], send_h, recv_h, to_m(peer))
-
-    each(nm - 1, send_hot)
-    h_in[block(member, slots), :] = h_out[block(member, slots), :]
-
     wait_bytes(ids_a.at[pl.ds(0, nyc - 1)], recv_ids.at[0])
     for peer in range(nyc):
         square[peer : peer + 1, :] = ids_a[peer]
@@ -263,6 +254,19 @@
 
     each(nz - 1, send_ids_z)
     ids_c[z] = ids_b[z]
+
+    wait_bytes(hot_ids.at[pl.ds(0, nm - 1)], recv_ids.at[2])
+    loads[5].wait()
+    for peer in range(nm):
+        wanted_rows = one_hot(lane_to_rows(hot_ids[peer], slots, 0), hot_ref.shape[0])
+        h_out[peer * slots : (peer + 1) * slots, :] = exact_dot(wanted_rows, hot_ref[...]).astype(bf16)
+
+    def send_hot(i):
+        peer = m_peer(i)
+        send(h_out.at[block(peer, slots)], h_in.at[block(member, slots)], send_h, recv_h, to_m(peer))
+
+    each(nm - 1, send_hot)
+    h_in[block(member, slots), :] = h_out[block(member, slots), :]
 
     rows_to = iota((ngroup, ngroup), 0)
     rows_from = iota((ngroup, ngroup), 1)
@@ -389,7 +393,7 @@
     x_send[...] = x_out[block(core, half), :] + x_core[...]
 
     def send_extra(i):
-        peer = lax.rem(y + 1 + i, ny)
+        peer = y_peer(i)
         send(x_send.at[block(peer, nz)], x_in.at[block(y, nz)], send_x.at[1], recv_x.at[1], to_yc(peer * 2 + core))
 
     each(ny - 1, send_extra)

time: 59.2 us -> 58.9 us (level)
  the two profiles are of different devices: /device:TPU:1 before, /device:TPU:6 now
where the time goes in v7:
time: 58.9 us; the launch traced here: 58.7 us
  Pallas kernels  57.9 us (98%)
  local copies, waits for them, and re-layouts  0.8 us (1%)
    pallas_call x1, Pallas kernels, per_device(): pl.pallas_call(functools.partial(layer_kernel, nz, nyc, nm), out_shape=pl...  57.9 us

profile of v7, /device:TPU:6, one launch (start us, length us, event | category | flops | bytes accessed | tf_op | source)
XLA Modules:
  0.0 58.7 jit_solution(13643033802777685260)
XLA Ops:
  0.0 57.9 %shard_map.109 = bf16[256,1024]{1,0:T(8,128)(2,1)S(1)} custom-call(bf16[256,768]{1,0:T(8,128)(2,1)} %targets_hbm.1, s32[25,256]{1,0:T(8,128)} %bitcast.1, bf16[512,768]{1,0:T(8,128)(2,1)} %hot_hbm.1, s32[1,1,4,64]{3,2,1,0:T(4,128)} %hot_req_hbm.1, s32[1,1,4]{2,1,0:T(1,128)} %live_hbm.1, bf16[512,768]{1,0:T(8,128)(2,1)} %table_hbm.1, s32[1,1,256]{2,1,0:T(1,128)} %owner_hbm.1, ...), custom_call_target="tpu_custom_call" | custom-call | flops 805306368 | bytes 8388608 | tf_op jit(solution)/shard_map/pallas_call | solution.py:484
  57.9 0.8 %copy.13 = bf16[256,1024]{1,0:T(8,128)(2,1)} copy(bf16[256,1024]{1,0:T(8,128)(2,1)S(1)} %shard_map.109) | data formatting | bytes 1048576

commit v8 on v7

--- a/solution.py
+++ b/solution.py
@@ -437,14 +437,8 @@
 
     def add_chunk(chunk, counts, rows_in):
         part = features_of(chunk)
-        aggregate = summed[:, part] + count_dot(counts, rows_in)
-        aggregate = (aggregate * (1.0 / FANOUT)).astype(bf16)
-        total[...] = total[...] + exact_dot(aggregate, w_neigh_ref[part, :])
-
-    wait_bytes(row_in.at[pl.ds(0, nz - 1)], recv_x.at[2])
-    for peer in range(nz):
-        extra[peer : peer + 1, :] = row_in[peer]
-    summed[...] = summed[...] + count_dot(second, extra[...].astype(bf16))
+        summed[:, part] = summed[:, part] + count_dot(counts, rows_in)
+
     wait_y(Z_FIRST[0])
     add_chunk(Z_FIRST[0], placed_turned, whole(y_in, Z_FIRST[0]))
     wait_z(Y_FIRST[0])
@@ -452,12 +446,22 @@
     for chunk in Z_FIRST[1:]:
         wait_y(chunk)
         add_chunk(chunk, placed_turned, whole(y_in, chunk))
-    for chunk in Y_FIRST[1:]:
+    for chunk in Y_FIRST[1:-1]:
         wait_z(chunk)
         add_chunk(chunk, placed, whole(z_in, chunk))
-    active = jnp.maximum(total[...], 0.0)
-    scale = lax.rsqrt(jnp.mean(active * active, axis=-1, keepdims=True) + 1e-06)
-    out_ref[...] = (active * scale).astype(bf16)
+    wait_bytes(row_in.at[pl.ds(0, nz - 1)], recv_x.at[2])
+    for peer in range(nz):
+        extra[peer : peer + 1, :] = row_in[peer]
+    summed[...] = summed[...] + count_dot(second, extra[...].astype(bf16))
+    wait_z(Y_FIRST[-1])
+    add_chunk(Y_FIRST[-1], placed, whole(z_in, Y_FIRST[-1]))
+    tile = rows // 2
+    for first_target in range(0, rows, tile):
+        part = slice(first_target, first_target + tile)
+        aggregate = (summed[part, :] * (1.0 / FANOUT)).astype(bf16)
+        active = jnp.maximum(total[part, :] + exact_dot(aggregate, w_neigh_ref[...]), 0.0)
+        scale = lax.rsqrt(jnp.mean(active * active, axis=-1, keepdims=True) + 1e-06)
+        out_ref[part, :] = (active * scale).astype(bf16)
 
     wait_bytes(ids_a.at[pl.ds(0, nyc - 1)], send_ids.at[0])
     wait_bytes(ids_c.at[pl.ds(0, nz - 1)], send_ids.at[1])

time: 58.9 us -> 57.8 us (0.981)
  Pallas kernels: 57.9 us -> 56.8 us
    pallas_call x1, Pallas kernels: 57.9 us -> 56.8 us  [per_device(): pl.pallas_call(functools.partial(layer_kernel, nz, nyc, nm), out_shape=pl...]
where the time goes in v8:
time: 57.8 us; the launch traced here: 57.6 us
  Pallas kernels  56.8 us (98%)
  local copies, waits for them, and re-layouts  0.8 us (1%)
    pallas_call x1, Pallas kernels, per_device(): pl.pallas_call(functools.partial(layer_kernel, nz, nyc, nm), out_shape=pl...  56.8 us

profile of v8, /device:TPU:6, one launch (start us, length us, event | category | flops | bytes accessed | tf_op | source)
XLA Modules:
  0.0 57.6 jit_solution(1961634031713374401)
XLA Ops:
  0.0 56.8 %shard_map.109 = bf16[256,1024]{1,0:T(8,128)(2,1)S(1)} custom-call(bf16[256,768]{1,0:T(8,128)(2,1)} %targets_hbm.1, s32[25,256]{1,0:T(8,128)} %bitcast.1, bf16[512,768]{1,0:T(8,128)(2,1)} %hot_hbm.1, s32[1,1,4,64]{3,2,1,0:T(4,128)} %hot_req_hbm.1, s32[1,1,4]{2,1,0:T(1,128)} %live_hbm.1, bf16[512,768]{1,0:T(8,128)(2,1)} %table_hbm.1, s32[1,1,256]{2,1,0:T(1,128)} %owner_hbm.1, ...), custom_call_target="tpu_custom_call" | custom-call | flops 805306368 | bytes 8388608 | tf_op jit(solution)/shard_map/pallas_call | solution.py:488
  56.8 0.8 %copy.13 = bf16[256,1024]{1,0:T(8,128)(2,1)} copy(bf16[256,1024]{1,0:T(8,128)(2,1)S(1)} %shard_map.109) | data formatting | bytes 1048576
